TPU v7x, 256 devices: a whole 4x4x8 slice. The times are simulated.
256 devices in a mesh: occi: 8 (over z_lo, y), occj: 32 (over x, z_hi, core).
Axes of the slice: x: 4, y: 4, z: 8 (z_hi: 4, z_lo: 2; z = z_hi * 2 + z_lo), core: 2. Of those that a mesh axis runs over, the one named last changes fastest.
Arguments:
- amplitudes: float32 [256, 768, 768], P(('occi', 'occj')), may hold values from -6 to 6
- first_rotation: float32 [768, 768], replicated, may hold values from -0.21875 to 0.21875
- second_rotation: float32 [768, 768], replicated, may hold values from -0.21875 to 0.21875
- pair_weights: float32 [16, 16], replicated, may hold values from -1.5 to 1.5
- denominators: float32 [16, 16, 768, 768], P('occi', None, 'occj'), may hold values from 1 to 4
Outputs:
- update: float32 [16, 16, 768, 768], P('occi', None, 'occj')
All inputs are finite; a program needn't handle non-finite values.
Results may differ from a plain program's by a relative error of at most 0.00007.
Values sent between devices are 32-bit elements; how exact they have to be, the bound alone decides.
No kernel may reach another device: no remote copies, remote signals or barrier semaphores. Data moves between devices by JAX's collectives and lax.ppermute only.
A program may use at most 64 MiB of HBM per device.

v0:
```python
import jax
import jax.numpy as jnp
from jax import lax
from jax.sharding import PartitionSpec as P

OCC = 16


def on_device(amplitudes, first_rotation, second_rotation, pair_weights, denominators):
    highest = lax.Precision.HIGHEST
    row_count = lax.axis_size("occi")
    column_count = lax.axis_size("occj")
    rows_here = OCC // row_count
    virtual = amplitudes.shape[1]
    slice_width = virtual // column_count
    halfway = jnp.einsum("ac,pcd->pad", first_rotation, amplitudes, precision=highest)
    finished = jnp.einsum("pad,bd->pab", halfway, second_rotation, precision=highest)
    outgoing = (jnp.swapaxes(finished, 1, 2), finished)
    direct, mirrored = (
        lax.all_to_all(outgoing[0], "occj", split_axis=1, concat_axis=0, tiled=True),
        lax.all_to_all(outgoing[1], "occj", split_axis=1, concat_axis=0, tiled=True),
    )
    direct = direct.reshape(rows_here, OCC, slice_width, virtual)
    mirrored = mirrored.reshape(rows_here, OCC, slice_width, virtual)
    mirrored = lax.all_to_all(mirrored, "occi", split_axis=1, concat_axis=0, tiled=True)
    summed = direct + jnp.swapaxes(mirrored, 0, 1)
    contracted = jnp.einsum("jk,ijba->ikba", pair_weights, summed, precision=highest)
    return contracted / denominators


def solution(mesh):
    placed = (P(("occi", "occj"), None, None), P(), P(), P(), P("occi", None, "occj", None))
    return jax.shard_map(
        on_device,
        mesh=mesh,
        in_specs=placed,
        out_specs=P("occi", None, "occj", None),
        check_vma=False,
    )
```

profile of v0, /device:TPU:1, one launch (start us, length us, event | category | flops | bytes accessed | tf_op | source)
XLA Modules:
  0.0 208.5 jit_solution(10778221006411062034)
XLA Ops:
  0.0 0.0 copy-start
  0.0 0.0 copy-start.3
  0.0 1.7 copy-done
  1.7 12.9 %fusion.2 = f32[768,768]{1,0:T(8,128)S(1)} fusion(f32[768,768]{1,0:T(8,128)S(1)} %copy-done, f32[1,768,768]{2,1,0:T(8,128)} %param.5), kind=kOutput, calls=%fused_computation.3 | convolution fusion | flops 5435817984 | bytes 7077888 | tf_op jit(solution)/shard_map/ac,pcd->pad/dot_general | solution.py:16
  14.5 0.0 copy-done.3
  14.6 11.7 %fusion = f32[768,768]{1,0:T(8,128)S(1)} fusion(f32[768,768]{1,0:T(8,128)S(1)} %copy-done.3, f32[768,768]{1,0:T(8,128)S(1)} %fusion.2), kind=kOutput, calls=%fused_computation | convolution fusion | flops 5435817984 | bytes 7077888 | tf_op jit(solution)/shard_map/pad,bd->pab/dot_general | solution.py:17
  26.3 0.0 copy-start.1
  26.3 1.4 copy-done.1
  27.7 3.8 %copy.18 = f32[1,768,768]{2,0,1:T(1,128)} copy(f32[1,768,768]{2,1,0:T(8,128)S(1)} %bitcast.28) | data formatting | bytes 4718592 | tf_op jit(solution)/shard_map/pad,bd->pab/dot_general | solution.py:17
  31.5 12.9 %all-to-all-start.1 = ((f32[1,768,768]{2,0,1:T(1,128)}), f32[1,768,768]{2,0,1:T(1,128)}, u32[]{:S(2)}, u32[]{:S(2)}) async-start(f32[1,768,768]{2,0,1:T(1,128)} %copy.18), calls=%async_computation.1 | async-start | bytes 4718592 | tf_op jit(solution)/shard_map/all_to_all | solution.py:21
  44.4 6.7 %copy.17 = f32[1,768,768]{2,0,1:T(1,128)} copy(f32[1,768,768]{1,2,0:T(8,128)} %bitcast.29) | data formatting | bytes 4718592 | tf_op jit(solution)/shard_map/transpose | solution.py:18
  51.1 49.4 %all-to-all-done.1 = f32[1,768,768]{2,0,1:T(1,128)} async-done(((f32[1,768,768]{2,0,1:T(1,128)}), f32[1,768,768]{2,0,1:T(1,128)}, u32[]{:S(2)}, u32[]{:S(2)}) %all-to-all-start.1) | async-done | bytes 2359328 | tf_op jit(solution)/shard_map/all_to_all | solution.py:21
  100.5 5.7 %all-to-all-start = ((f32[1,768,768]{2,0,1:T(1,128)}), f32[1,768,768]{2,0,1:T(1,128)}, u32[]{:S(2)}, u32[]{:S(2)}) async-start(f32[1,768,768]{2,0,1:T(1,128)} %copy.17), calls=%async_computation | async-start | bytes 4718592 | tf_op jit(solution)/shard_map/all_to_all | solution.py:20
  106.3 1.8 copy.28
  108.1 1.7 copy.19
  109.8 45.5 %all-to-all-done = f32[1,768,768]{2,0,1:T(1,128)} async-done(((f32[1,768,768]{2,0,1:T(1,128)}), f32[1,768,768]{2,0,1:T(1,128)}, u32[]{:S(2)}, u32[]{:S(2)}) %all-to-all-start) | async-done | bytes 2359328 | tf_op jit(solution)/shard_map/all_to_all | solution.py:20
  155.2 14.0 %all-to-all-start.2 = ((f32[2,16,24,768]{3,2,0,1:T(8,128)}), f32[2,16,24,768]{3,2,0,1:T(8,128)}, u32[]{:S(2)}, u32[]{:S(2)}) async-start(f32[2,16,24,768]{3,2,0,1:T(8,128)} %copy.19), calls=%async_computation.2 | async-start | bytes 4718592 | tf_op jit(solution)/shard_map/all_to_all | solution.py:25
  169.2 3.2 %copy.27 = f32[1,768,768]{2,1,0:T(8,128)} copy(f32[1,768,768]{2,0,1:T(1,128)} %all-to-all-done) | data formatting | bytes 4718592
  172.4 25.8 %all-to-all-done.2 = f32[2,16,24,768]{3,2,0,1:T(8,128)} async-done(((f32[2,16,24,768]{3,2,0,1:T(8,128)}), f32[2,16,24,768]{3,2,0,1:T(8,128)}, u32[]{:S(2)}, u32[]{:S(2)}) %all-to-all-start.2) | async-done | bytes 2359328 | tf_op jit(solution)/shard_map/all_to_all | solution.py:25
  198.3 0.0 copy-start.2
  198.3 2.0 copy.20
  200.2 0.4 copy-done.2
  200.6 0.0 copy-start.4
  200.6 0.0 copy-start.5
  200.6 0.3 add.3
  200.9 1.4 copy-done.4
  202.3 0.0 copy-done.5
  202.3 3.4 %bitcast_divide_fusion = f32[2,16,24,768]{3,1,2,0:T(8,128)S(1)} fusion(f32[2,16,24,768]{3,2,1,0:T(8,128)S(1)} %copy-done.4, f32[2,16,24,768]{3,2,1,0:T(8,128)S(1)} %add.3, f32[16,16]{1,0:T(8,128)S(1)} %copy-done.5), kind=kOutput, calls=%fused_computation.2 | convolution fusion | flops 113836032 | bytes 7078912 | tf_op jit(solution)/shard_map/jk,ijba->ikba/dot_general | solution.py:27
  205.8 2.8 %copy.24 = f32[2,16,24,768]{3,2,1,0:T(8,128)} copy(f32[2,16,24,768]{3,1,2,0:T(8,128)S(1)} %bitcast_divide_fusion) | data formatting | bytes 4718592 | tf_op jit(solution)/shard_map/div | solution.py:28
Async XLA Ops:
  0.0 1.7 copy-start
  0.0 14.5 %copy-start.3 = (f32[768,768]{1,0:T(8,128)S(1)}, f32[768,768]{1,0:T(8,128)}, u32[]{:S(2)}) copy-start(f32[768,768]{1,0:T(8,128)} %param.7) | copy-start | bytes 7077892
  26.3 1.4 copy-start.1
  31.5 69.0 %all-to-all-start.1 = ((f32[1,768,768]{2,0,1:T(1,128)}), f32[1,768,768]{2,0,1:T(1,128)}, u32[]{:S(2)}, u32[]{:S(2)}) async-start(f32[1,768,768]{2,0,1:T(1,128)} %copy.18), calls=%async_computation.1 | async-start | bytes 4718592 | tf_op jit(solution)/shard_map/all_to_all | solution.py:21
  100.5 54.7 %all-to-all-start = ((f32[1,768,768]{2,0,1:T(1,128)}), f32[1,768,768]{2,0,1:T(1,128)}, u32[]{:S(2)}, u32[]{:S(2)}) async-start(f32[1,768,768]{2,0,1:T(1,128)} %copy.17), calls=%async_computation | async-start | bytes 4718592 | tf_op jit(solution)/shard_map/all_to_all | solution.py:20
  155.2 43.0 %all-to-all-start.2 = ((f32[2,16,24,768]{3,2,0,1:T(8,128)}), f32[2,16,24,768]{3,2,0,1:T(8,128)}, u32[]{:S(2)}, u32[]{:S(2)}) async-start(f32[2,16,24,768]{3,2,0,1:T(8,128)} %copy.19), calls=%async_computation.2 | async-start | bytes 4718592 | tf_op jit(solution)/shard_map/all_to_all | solution.py:25
  198.3 2.4 %copy-start.2 = (f32[1,768,768]{2,1,0:T(8,128)S(1)}, f32[1,768,768]{2,1,0:T(8,128)}, u32[]{:S(2)}) copy-start(f32[1,768,768]{2,1,0:T(8,128)} %copy.27) | copy-start | bytes 7077892
  200.6 1.7 copy-start.4
  200.6 1.7 copy-start.5
where the time goes:
time: 209 us
  waiting for transfers between devices  121 us (58%)
  starting transfers between devices  32.6 us (16%)
  matrix products  28 us (13%)
  local copies, waits for them, and re-layouts  26.9 us (13%)
    all_to_all x1, waiting for transfers between devices, on_device(): lax.all_to_all(outgoing[1], 'occj', split_axis=1, concat_axis=0, tiled=True)  49.4 us
    all_to_all x1, waiting for transfers between devices, on_device(): lax.all_to_all(outgoing[0], 'occj', split_axis=1, concat_axis=0, tiled=True)  45.5 us
    all_to_all x1, waiting for transfers between devices, on_device(): lax.all_to_all(mirrored, 'occi', split_axis=1, concat_axis=0, tiled=True)  25.8 us
    all_to_all x1, starting transfers between devices, on_device(): lax.all_to_all(mirrored, 'occi', split_axis=1, concat_axis=0, tiled=True)  14 us
    dot_general x1, matrix products, on_device(): jnp.einsum('ac,pcd->pad', first_rotation, amplitudes, precision=highest)  12.9 us
    all_to_all x1, starting transfers between devices, on_device(): lax.all_to_all(outgoing[1], 'occj', split_axis=1, concat_axis=0, tiled=True)  12.9 us
    dot_general x1, matrix products, on_device(): jnp.einsum('pad,bd->pab', halfway, second_rotation, precision=highest)  11.7 us
    unnamed x14, local copies, waits for them, and re-layouts  9.88 us
  transfers between devices with their start and end apart: 3, of which 3 were waited for; matrix products, arithmetic and copies ran while one was open for 6% of the time, Pallas kernels for 0%

commit v1 on v0

v1 whole, which is shorter than its diff:
```python
import jax
import jax.numpy as jnp
from jax import lax
from jax.experimental import pallas as pl
from jax.experimental.pallas import tpu as pltpu
from jax.sharding import PartitionSpec as P

OCC = 16
VIRT = 768
ROWS = 8
COLS = 32
WIDTH = VIRT // COLS
HALF = VIRT // 2
CHUNK = 256
F32 = jnp.float32
BF16 = jnp.bfloat16
NT = (((1,), (1,)), ((), ()))
NN = (((1,), (0,)), ((), ()))


def halves(x):
    high = x.astype(BF16)
    return high, (x - high.astype(F32)).astype(BF16)


def dot3(lh, ll, rh, rl, dims):
    def one(a, b):
        return lax.dot_general(a, b, dims, preferred_element_type=F32)

    return one(lh, rh) + (one(lh, rl) + one(ll, rh))


def transform_kernel(mode_ref, t_ref, a_ref, b_ref, z_ref, th, tl, bh, bl, hh, hl):
    mode = mode_ref[0]

    @pl.loop(0, VIRT // CHUNK)
    def _(i):
        rows = pl.ds(pl.multiple_of(i * CHUNK, CHUNK), CHUNK)
        th[rows, :], tl[rows, :] = halves(t_ref[rows, :])
        bh[rows, :], bl[rows, :] = halves(b_ref[rows, :])

    @pl.loop(0, VIRT // CHUNK)
    def _(i):
        rows = pl.ds(pl.multiple_of(i * CHUNK, CHUNK), CHUNK)
        ah, al = halves(a_ref[rows, :])
        hh[rows, :], hl[rows, :] = halves(dot3(ah, al, th[...], tl[...], NN))

    @pl.when(mode == 0)
    def _():
        @pl.loop(0, VIRT // CHUNK)
        def _(i):
            rows = pl.ds(pl.multiple_of(i * CHUNK, CHUNK), CHUNK)
            z_ref[rows, :] = dot3(bh[rows, :], bl[rows, :], hh[...], hl[...], NT)

    @pl.when(mode != 0)
    def _():
        @pl.loop(0, VIRT // CHUNK)
        def _(i):
            rows = pl.ds(pl.multiple_of(i * CHUNK, CHUNK), CHUNK)
            z_ref[rows, :] = dot3(hh[rows, :], hl[rows, :], bh[...], bl[...], NT)

    @pl.when(mode == 2)
    def _():
        @pl.loop(0, VIRT // CHUNK)
        def _(i):
            rows = pl.ds(pl.multiple_of(i * CHUNK, CHUNK), CHUNK)
            other = dot3(bh[rows, :], bl[rows, :], hh[...], hl[...], NT)
            z_ref[rows, :] = 0.5 * (z_ref[rows, :] + other)


def transform(mode, t, a, b):
    vmem = pl.BlockSpec(memory_space=pltpu.VMEM)
    return pl.pallas_call(
        transform_kernel,
        out_shape=jax.ShapeDtypeStruct((VIRT, VIRT), F32),
        in_specs=[pl.BlockSpec(memory_space=pltpu.SMEM), vmem, vmem, vmem],
        out_specs=vmem,
        scratch_shapes=[pltpu.VMEM((VIRT, VIRT), BF16)] * 6,
        compiler_params=pltpu.CompilerParams(vmem_limit_bytes=40 * 2**20),
        name="transform",
    )(mode, t, a, b)


LOST = (
    [(p0, 7, q0) for p0 in range(2) for q0 in range(2)]
    + [(p0, 6, q0) for p0 in range(2) for q0 in range(2)]
    + [(p0, 5, q0) for p0 in range(2) for q0 in range(2)]
    + [(1, 0, 0), (0, 4, 1), (0, 4, 0), (1, 4, 1)]
)


def item(z_ref, got, row, p0, step, q0):
    own = z_ref[p0, lax.rem(row + step, ROWS), q0]
    if step == 0:
        return own + z_ref[q0, row, p0]
    return own + got[step][q0, p0]


def lost_kernel(row_ref, z_ref, g7, g6, g5, g4, o_ref, stage):
    row = row_ref[0]
    got = {7: g7, 6: g6, 5: g5, 4: g4}
    for n, (p0, step, q0) in enumerate(LOST):
        stage[n * WIDTH : (n + 1) * WIDTH, :] = item(z_ref, got, row, p0, step, q0)
    for i in range(HALF // 128):
        o_ref[:, i * 128 : (i + 1) * 128] = stage[i * 128 : (i + 1) * 128, :].T


def lost_items(row, z, g7, g6, g5, g4):
    vmem = pl.BlockSpec(memory_space=pltpu.VMEM)
    return pl.pallas_call(
        lost_kernel,
        out_shape=jax.ShapeDtypeStruct((VIRT, HALF), F32),
        in_specs=[pl.BlockSpec(memory_space=pltpu.SMEM)] + [vmem] * 5,
        out_specs=vmem,
        scratch_shapes=[pltpu.VMEM((HALF, VIRT), F32)],
        compiler_params=pltpu.CompilerParams(vmem_limit_bytes=40 * 2**20),
        name="lost_items",
    )(row, z, g7, g6, g5, g4)


def finish_kernel(row_ref, z_ref, g4, g3, g2, g1, back_ref, w_ref, d_ref, o_ref, tiles, s_ref):
    row = row_ref[0]
    got = {4: g4, 3: g3, 2: g2, 1: g1}
    group = lax.broadcasted_iota(jnp.int32, (WIDTH, HALF), 1) // WIDTH
    for bit in (1, 2, 4, 8):
        upper = (group // bit) % 2 == 1
        for half in range(2):
            for c in range(16):
                if c & bit:
                    continue
                if bit == 1:
                    low = back_ref[half * 16 + c]
                    high = back_ref[half * 16 + c + bit]
                else:
                    low = tiles[half, c]
                    high = tiles[half, c + bit]
                tiles[half, c] = jnp.where(upper, pltpu.roll(high, bit * WIDTH, 1), low)
                tiles[half, c + bit] = jnp.where(upper, high, pltpu.roll(low, HALF - bit * WIDTH, 1))
    place = {key: n for n, key in enumerate(LOST)}
    for p0 in range(2):
        for step in range(ROWS):
            for q0 in range(2):
                n = step * 2 + q0
                key = (p0, step, q0)
                tie = step == 4 and p0 == q0
                if key not in place or tie:
                    kept = item(z_ref, got, row, p0, step, q0)
                for half in range(2):
                    lanes = slice(half * HALF, (half + 1) * HALF)
                    if key not in place:
                        s_ref[p0, n, :, lanes] = kept[:, lanes]
                    elif tie:
                        s_ref[p0, n, :, lanes] = jnp.where(
                            row < ROWS // 2, kept[:, lanes], tiles[half, place[key]]
                        )
                    else:
                        s_ref[p0, n, :, lanes] = tiles[half, place[key]]
    wh, wl = halves(w_ref[...])
    for p0 in range(2):
        for g in range(WIDTH // 8):
            rows = slice(g * 8, (g + 1) * 8)
            sh, sl = halves(s_ref[p0, :, rows, :].reshape(OCC * 8, VIRT))
            total = dot3(wh, wl, sh, sl, NN).reshape(OCC, 8, VIRT)
            o_ref[p0, :, rows, :] = total / d_ref[p0, :, rows, :]


def finish(row, z, g4, g3, g2, g1, back, w, d):
    vmem = pl.BlockSpec(memory_space=pltpu.VMEM)
    return pl.pallas_call(
        finish_kernel,
        out_shape=jax.ShapeDtypeStruct(d.shape, F32),
        in_specs=[pl.BlockSpec(memory_space=pltpu.SMEM)] + [vmem] * 8,
        out_specs=vmem,
        scratch_shapes=[
            pltpu.VMEM((2, OCC, WIDTH, HALF), F32),
            pltpu.VMEM((2, OCC, WIDTH, VIRT), F32),
        ],
        compiler_params=pltpu.CompilerParams(vmem_limit_bytes=48 * 2**20),
        name="finish",
    )(row, z, g4, g3, g2, g1, back, w, d)


def on_device(amplitudes, first_rotation, second_rotation, pair_weights, denominators):
    row = lax.axis_index("occi")
    column = lax.axis_index("occj")
    p = 2 * row + column // OCC
    ahead = jnp.mod(column % OCC - p, OCC)
    wins = ((ahead >= 1) & (ahead <= 7)) | ((ahead == 8) & (p < 8))
    mode = jnp.where(ahead == 0, 2, jnp.where(wins, 0, 1)).astype(jnp.int32).reshape(1)
    row_here = row.astype(jnp.int32).reshape(1)

    turned = jnp.roll(pair_weights, -2 * row, axis=0)
    spread = jnp.einsum("jk,xy->kxjy", turned, jnp.eye(8, dtype=F32), precision="highest").reshape(128, 128)

    z = transform(mode, amplitudes[0], first_rotation, second_rotation)
    z = lax.all_to_all(z.reshape(COLS, WIDTH, VIRT), "occj", split_axis=0, concat_axis=0, tiled=True)
    z = z.reshape(2, ROWS, 2, WIDTH, VIRT)

    def exchange(step):
        out = lax.dynamic_index_in_dim(z, jnp.mod(row + step, ROWS), 1, keepdims=False)
        return lax.ppermute(out, "occi", [(r, (r + step) % ROWS) for r in range(ROWS)])

    got = {ROWS - step: exchange(step) for step in range(1, ROWS)}
    lost = lost_items(row_here, z, got[7], got[6], got[5], got[4])
    back = lax.all_to_all(lost.reshape(COLS, WIDTH, HALF), "occj", split_axis=0, concat_axis=0, tiled=True)
    return finish(row_here, z, got[4], got[3], got[2], got[1], back, spread, denominators)


def solution(mesh):
    placed = (P(("occi", "occj"), None, None), P(), P(), P(), P("occi", None, "occj", None))
    return jax.shard_map(
        on_device,
        mesh=mesh,
        in_specs=placed,
        out_specs=P("occi", None, "occj", None),
        check_vma=False,
    )
```

time: 209 us -> 173 us (0.83)
  matrix products: 28 us -> 0 us
  waiting for transfers between devices: 121 us -> 107 us
  local copies, waits for them, and re-layouts: 26.9 us -> 12.9 us
  Pallas kernels: 0 us -> 13.1 us
  starting transfers between devices: 32.6 us -> 36.6 us
  other arithmetic: 0.29 us -> 2.42 us
    all_to_all x3 -> x2, waiting for transfers between devices: 121 us -> 55.8 us  [the longest x1 55.8 us: on_device(): lax.all_to_all(z.reshape(COLS, WIDTH, VIRT), 'occj', split_axis=0, concat...]
    ppermute x0 -> x7, waiting for transfers between devices: none -> 51.3 us  [exchange(): lax.ppermute(out, 'occi', [(r, (r + step) % ROWS) for r in range(ROWS)])]
    dot_general x3 -> x0, matrix products: 28 us -> none  [the longest x1 12.9 us: on_device(): jnp.einsum('ac,pcd->pad', first_rotation, amplitudes, precision=highest)]
    ppermute x0 -> x7, starting transfers between devices: none -> 15.5 us  [exchange(): lax.ppermute(out, 'occi', [(r, (r + step) % ROWS) for r in range(ROWS)])]
    pallas_call x0 -> x3, Pallas kernels: none -> 13.1 us  [the longest x1 7.38 us: transform(): pl.pallas_call(transform_kernel, out_shape=jax.ShapeDtypeStruct((VIRT, VI...]
    all_to_all x3 -> x2, starting transfers between devices: 32.6 us -> 21.1 us  [the longest x1 12.6 us: on_device(): lax.all_to_all(z.reshape(COLS, WIDTH, VIRT), 'occj', split_axis=0, concat...]
    transpose x1 -> x0, local copies, waits for them, and re-layouts: 6.72 us -> none  [on_device(): outgoing = (jnp.swapaxes(finished, 1, 2), finished)]
    dot_general x1 -> x0, local copies, waits for them, and re-layouts: 3.83 us -> none  [on_device(): jnp.einsum('pad,bd->pab', halfway, second_rotation, precision=highest)]
  transfers between devices with their start and end apart: 3 -> 9, of which waited for: 3 -> 6; matrix products, arithmetic and copies ran while one was open for 6% -> 3% of each run, Pallas kernels for 0% -> 0%
where the time goes in v1:
time: 173 us; the launch traced here: 172 us
  waiting for transfers between devices  107 us (62%)
  starting transfers between devices  36.6 us (21%)
  Pallas kernels  13.1 us (8%)
  local copies, waits for them, and re-layouts  12.9 us (7%)
  other arithmetic  2.42 us (1%)
    all_to_all x1, waiting for transfers between devices, on_device(): lax.all_to_all(z.reshape(COLS, WIDTH, VIRT), 'occj', split_axis=0, concat...  55.8 us
    ppermute x7, waiting for transfers between devices, exchange(): lax.ppermute(out, 'occi', [(r, (r + step) % ROWS) for r in range(ROWS)])  51.3 us
    ppermute x7, starting transfers between devices, exchange(): lax.ppermute(out, 'occi', [(r, (r + step) % ROWS) for r in range(ROWS)])  15.5 us
    all_to_all x1, starting transfers between devices, on_device(): lax.all_to_all(z.reshape(COLS, WIDTH, VIRT), 'occj', split_axis=0, concat...  12.6 us
    unnamed x18, local copies, waits for them, and re-layouts  9.56 us
    all_to_all x1, starting transfers between devices, on_device(): lax.all_to_all(lost.reshape(COLS, WIDTH, HALF), 'occj', split_axis=0, con...  8.46 us
    pallas_call x1, Pallas kernels, transform(): pl.pallas_call(transform_kernel, out_shape=jax.ShapeDtypeStruct((VIRT, VI...  7.38 us
    pallas_call x1, Pallas kernels, finish(): pl.pallas_call(finish_kernel, out_shape=jax.ShapeDtypeStruct(d.shape, F32...  5.31 us
  transfers between devices with their start and end apart: 9, of which 6 were waited for; matrix products, arithmetic and copies ran while one was open for 3% of the time, Pallas kernels for 0%

profile of v1, /device:TPU:1, one launch (start us, length us, event | category | flops | bytes accessed | tf_op | source)
XLA Modules:
  0.0 172.3 jit_solution(4096761554406180122)
XLA Ops:
  0.0 1.7 copy-done.2
  1.7 1.7 copy-done.3
  3.3 1.7 copy-done.4
  5.0 7.4 %transform.1 = f32[768,768]{1,0:T(8,128)S(1)} custom-call(s32[1]{0:T(128)} %bitcast.1.mode_ref, f32[768,768]{1,0:T(8,128)S(1)} %bitcast.29, f32[768,768]{1,0:T(8,128)S(1)} %copy-done.3, f32[768,768]{1,0:T(8,128)S(1)} %copy-done.4), custom_call_target="tpu_custom_call" | custom-call | tf_op jit(solution)/shard_map/transform/pallas_call | solution.py:73
  12.4 0.0 copy-start
  12.4 1.4 copy-done
  13.8 12.6 %all-to-all-start = ((f32[32,24,768]{2,1,0:T(8,128)}), f32[32,24,768]{2,1,0:T(8,128)S(1)}, u32[]{:S(2)}, u32[]{:S(2)}) async-start(f32[32,24,768]{2,1,0:T(8,128)} %bitcast.27), calls=%async_computation | async-start | bytes 4718592 | tf_op jit(solution)/shard_map/all_to_all | solution.py:196
  26.5 55.8 %all-to-all-done = f32[32,24,768]{2,1,0:T(8,128)S(1)} async-done(((f32[32,24,768]{2,1,0:T(8,128)}), f32[32,24,768]{2,1,0:T(8,128)S(1)}, u32[]{:S(2)}, u32[]{:S(2)}) %all-to-all-start) | async-done | bytes 2359328 | tf_op jit(solution)/shard_map/all_to_all | solution.py:196
  82.3 1.0 dynamic-slice_bitcast_fusion
  83.3 6.0 %collective-permute-start.6 = (f32[2,2,24,768]{3,2,1,0:T(8,128)S(1)}, f32[2,2,24,768]{3,2,1,0:T(8,128)S(1)}, u32[]{:S(2)}, u32[]{:S(2)}) collective-permute-start(f32[2,2,24,768]{3,2,1,0:T(8,128)S(1)} %get-tuple-element.5), channel_id=1, source_target_pairs={{0,96},{32,128},{64,160},{96,192},{128,224},{160,0},{192,32},{224,... | collective-permute-start | bytes 884744 | tf_op jit(solution)/shard_map/ppermute | solution.py:201
  89.3 1.1 collective-permute-start.5
  90.4 0.0 collective-permute-start.4
  90.4 2.0 %collective-permute-start = (f32[2,2,24,768]{3,2,1,0:T(8,128)S(1)}, f32[2,2,24,768]{3,2,1,0:T(8,128)S(1)}, u32[]{:S(2)}, u32[]{:S(2)}) collective-permute-start(f32[2,2,24,768]{3,2,1,0:T(8,128)S(1)} %get-tuple-element.11), channel_id=1, source_target_pairs={{0,128},{32,160},{64,192},{96,224},{128,0},{160,32},{192,64},{224,... | collective-permute-start | bytes 884744 | tf_op jit(solution)/shard_map/ppermute | solution.py:201
  92.4 8.1 %collective-permute-done.6.g5 = f32[2,2,24,768]{3,2,1,0:T(8,128)S(1)} collective-permute-done((f32[2,2,24,768]{3,2,1,0:T(8,128)S(1)}, f32[2,2,24,768]{3,2,1,0:T(8,128)S(1)}, u32[]{:S(2)}, u32[]{:S(2)}) %collective-permute-start.6) | collective-permute-done | bytes 294944 | tf_op jit(solution)/shard_map/ppermute | solution.py:201
  100.6 0.0 collective-permute-done.5.g6
  100.6 9.4 %collective-permute-done.4.g7 = f32[2,2,24,768]{3,2,1,0:T(8,128)S(1)} collective-permute-done((f32[2,2,24,768]{3,2,1,0:T(8,128)S(1)}, f32[2,2,24,768]{3,2,1,0:T(8,128)S(1)}, u32[]{:S(2)}, u32[]{:S(2)}) %collective-permute-start.4) | collective-permute-done | bytes 294944 | tf_op jit(solution)/shard_map/ppermute | solution.py:201
  109.9 0.4 lost_items.1
  110.3 0.3 copy-done.5
  110.7 1.0 copy-done.1
  111.7 8.5 %all-to-all-start.1 = ((f32[32,24,384]{2,1,0:T(8,128)}), f32[32,24,384]{2,1,0:T(8,128)S(1)}, u32[]{:S(2)}, u32[]{:S(2)}) async-start(f32[32,24,384]{2,1,0:T(8,128)} %bitcast.28), calls=%async_computation.1 | async-start | bytes 2359296 | tf_op jit(solution)/shard_map/all_to_all | solution.py:205
  120.2 4.6 %collective-permute-start.3 = (f32[2,2,24,768]{3,2,1,0:T(8,128)}, f32[2,2,24,768]{3,2,1,0:T(8,128)}, u32[]{:S(2)}, u32[]{:S(2)}) collective-permute-start(f32[2,2,24,768]{3,2,1,0:T(8,128)} %get-tuple-element.8), channel_id=1, source_target_pairs={{0,224},{32,0},{64,32},{96,64},{128,96},{160,128},{192,160},{224,1... | collective-permute-start | bytes 884744 | tf_op jit(solution)/shard_map/ppermute | solution.py:201
  124.8 1.8 %collective-permute-start.1 = (f32[2,2,24,768]{3,2,1,0:T(8,128)}, f32[2,2,24,768]{3,2,1,0:T(8,128)}, u32[]{:S(2)}, u32[]{:S(2)}) collective-permute-start(f32[2,2,24,768]{3,2,1,0:T(8,128)} %get-tuple-element.10), channel_id=1, source_target_pairs={{0,160},{32,192},{64,224},{96,0},{128,32},{160,64},{192,96},{224,1... | collective-permute-start | bytes 884744 | tf_op jit(solution)/shard_map/ppermute | solution.py:201
  126.6 0.6 fusion.1
  127.2 0.1 copy.7
  127.3 1.8 %multiply_bitcast_fusion = f32[16,8,16,8]{3,2,1,0:T(8,128)} fusion(f32[16,16]{0,1:T(8,128)S(1)} %copy.7, f32[8,8]{1,0:T(8,128)} %fusion.1), kind=kLoop, calls=%fused_computation | loop fusion | flops 16384 | bytes 66816 | tf_op jit(solution)/shard_map/jk,xy->kxjy/transpose | solution.py:193
  129.1 2.3 %reshape.23.w_ref = f32[128,128]{1,0:T(8,128)} reshape(f32[16,8,16,8]{3,2,1,0:T(8,128)} %multiply_bitcast_fusion) | data formatting | bytes 131072 | tf_op jit(solution)/shard_map/reshape | solution.py:193
  131.4 21.2 %collective-permute-done.3.g1 = f32[2,2,24,768]{3,2,1,0:T(8,128)} collective-permute-done((f32[2,2,24,768]{3,2,1,0:T(8,128)}, f32[2,2,24,768]{3,2,1,0:T(8,128)}, u32[]{:S(2)}, u32[]{:S(2)}) %collective-permute-start.3) | collective-permute-done | bytes 294944 | tf_op jit(solution)/shard_map/ppermute | solution.py:201
  152.6 6.3 %collective-permute-done.2.g2 = f32[2,2,24,768]{3,2,1,0:T(8,128)} collective-permute-done((f32[2,2,24,768]{3,2,1,0:T(8,128)}, f32[2,2,24,768]{3,2,1,0:T(8,128)}, u32[]{:S(2)}, u32[]{:S(2)}) %collective-permute-start.2) | collective-permute-done | bytes 294944 | tf_op jit(solution)/shard_map/ppermute | solution.py:201
  158.9 6.3 %collective-permute-done.1.g3 = f32[2,2,24,768]{3,2,1,0:T(8,128)} collective-permute-done((f32[2,2,24,768]{3,2,1,0:T(8,128)}, f32[2,2,24,768]{3,2,1,0:T(8,128)}, u32[]{:S(2)}, u32[]{:S(2)}) %collective-permute-start.1) | collective-permute-done | bytes 294944 | tf_op jit(solution)/shard_map/ppermute | solution.py:201
  165.2 1.0 copy-done.6
  166.2 0.8 copy-done.7
  167.0 5.3 %finish.1 = f32[2,16,24,768]{3,2,1,0:T(8,128)} custom-call(s32[1]{0:T(128)} %bitcast.row_ref, f32[2,8,2,24,768]{4,3,2,1,0:T(8,128)S(1)} %bitcast.26, f32[2,2,24,768]{3,2,1,0:T(8,128)S(1)} %copy-done.6, f32[2,2,24,768]{3,2,1,0:T(8,128)} %collective-permute-done.1.g3, f32[2,2,24,768]{3,2,1,0:T(8,128)} %collective-permute-done.2.g2, ...), custom_call_target="tpu_custom_call" | custom-call | tf_op jit(solution)/shard_map/finish/pallas_call | solution.py:169
  (13 shorter events, 0.0 us)
Async XLA Ops:
  0.0 1.7 copy-start.2
  1.7 1.7 copy-start.3
  3.3 1.7 copy-start.4
  12.4 1.4 copy-start
  13.8 68.6 %all-to-all-start = ((f32[32,24,768]{2,1,0:T(8,128)}), f32[32,24,768]{2,1,0:T(8,128)S(1)}, u32[]{:S(2)}, u32[]{:S(2)}) async-start(f32[32,24,768]{2,1,0:T(8,128)} %bitcast.27), calls=%async_computation | async-start | bytes 4718592 | tf_op jit(solution)/shard_map/all_to_all | solution.py:196
  83.3 17.2 %collective-permute-start.6 = (f32[2,2,24,768]{3,2,1,0:T(8,128)S(1)}, f32[2,2,24,768]{3,2,1,0:T(8,128)S(1)}, u32[]{:S(2)}, u32[]{:S(2)}) collective-permute-start(f32[2,2,24,768]{3,2,1,0:T(8,128)S(1)} %get-tuple-element.5), channel_id=1, source_target_pairs={{0,96},{32,128},{64,160},{96,192},{128,224},{160,0},{192,32},{224,... | collective-permute-start | bytes 884744 | tf_op jit(solution)/shard_map/ppermute | solution.py:201
  89.3 11.3 %collective-permute-start.5 = (f32[2,2,24,768]{3,2,1,0:T(8,128)S(1)}, f32[2,2,24,768]{3,2,1,0:T(8,128)S(1)}, u32[]{:S(2)}, u32[]{:S(2)}) collective-permute-start(f32[2,2,24,768]{3,2,1,0:T(8,128)S(1)} %get-tuple-element.6), channel_id=1, source_target_pairs={{0,64},{32,96},{64,128},{96,160},{128,192},{160,224},{192,0},{224,... | collective-permute-start | bytes 884744 | tf_op jit(solution)/shard_map/ppermute | solution.py:201
  90.4 19.5 %collective-permute-start.4 = (f32[2,2,24,768]{3,2,1,0:T(8,128)S(1)}, f32[2,2,24,768]{3,2,1,0:T(8,128)S(1)}, u32[]{:S(2)}, u32[]{:S(2)}) collective-permute-start(f32[2,2,24,768]{3,2,1,0:T(8,128)S(1)} %get-tuple-element.7), channel_id=1, source_target_pairs={{0,32},{32,64},{64,96},{96,128},{128,160},{160,192},{192,224},{224... | collective-permute-start | bytes 884744 | tf_op jit(solution)/shard_map/ppermute | solution.py:201
  90.4 19.5 %collective-permute-start = (f32[2,2,24,768]{3,2,1,0:T(8,128)S(1)}, f32[2,2,24,768]{3,2,1,0:T(8,128)S(1)}, u32[]{:S(2)}, u32[]{:S(2)}) collective-permute-start(f32[2,2,24,768]{3,2,1,0:T(8,128)S(1)} %get-tuple-element.11), channel_id=1, source_target_pairs={{0,128},{32,160},{64,192},{96,224},{128,0},{160,32},{192,64},{224,... | collective-permute-start | bytes 884744 | tf_op jit(solution)/shard_map/ppermute | solution.py:201
  109.9 0.7 copy-start.5
  110.6 1.0 copy-start.1
  111.7 8.5 %copy-start.8 = (f32[16,16]{1,0:T(8,128)S(1)}, f32[16,16]{1,0:T(8,128)}, u32[]{:S(2)}) copy-start(f32[16,16]{1,0:T(8,128)} %param.8) | copy-start | bytes 3076
  111.7 53.6 %all-to-all-start.1 = ((f32[32,24,384]{2,1,0:T(8,128)}), f32[32,24,384]{2,1,0:T(8,128)S(1)}, u32[]{:S(2)}, u32[]{:S(2)}) async-start(f32[32,24,384]{2,1,0:T(8,128)} %bitcast.28), calls=%async_computation.1 | async-start | bytes 2359296 | tf_op jit(solution)/shard_map/all_to_all | solution.py:205
  120.2 32.4 %collective-permute-start.3 = (f32[2,2,24,768]{3,2,1,0:T(8,128)}, f32[2,2,24,768]{3,2,1,0:T(8,128)}, u32[]{:S(2)}, u32[]{:S(2)}) collective-permute-start(f32[2,2,24,768]{3,2,1,0:T(8,128)} %get-tuple-element.8), channel_id=1, source_target_pairs={{0,224},{32,0},{64,32},{96,64},{128,96},{160,128},{192,160},{224,1... | collective-permute-start | bytes 884744 | tf_op jit(solution)/shard_map/ppermute | solution.py:201
  124.8 34.1 %collective-permute-start.2 = (f32[2,2,24,768]{3,2,1,0:T(8,128)}, f32[2,2,24,768]{3,2,1,0:T(8,128)}, u32[]{:S(2)}, u32[]{:S(2)}) collective-permute-start(f32[2,2,24,768]{3,2,1,0:T(8,128)} %get-tuple-element.9), channel_id=1, source_target_pairs={{0,192},{32,224},{64,0},{96,32},{128,64},{160,96},{192,128},{224,1... | collective-permute-start | bytes 884744 | tf_op jit(solution)/shard_map/ppermute | solution.py:201
  124.8 40.4 %collective-permute-start.1 = (f32[2,2,24,768]{3,2,1,0:T(8,128)}, f32[2,2,24,768]{3,2,1,0:T(8,128)}, u32[]{:S(2)}, u32[]{:S(2)}) collective-permute-start(f32[2,2,24,768]{3,2,1,0:T(8,128)} %get-tuple-element.10), channel_id=1, source_target_pairs={{0,160},{32,192},{64,224},{96,0},{128,32},{160,64},{192,96},{224,1... | collective-permute-start | bytes 884744 | tf_op jit(solution)/shard_map/ppermute | solution.py:201
  165.2 1.0 copy-start.6
  166.2 0.8 copy-start.7

commit v2 on v0

v2 whole, which is shorter than its diff:
```python
import jax
import jax.numpy as jnp
from jax import lax
from jax.experimental import pallas as pl
from jax.experimental.pallas import tpu as pltpu
from jax.sharding import PartitionSpec as P

OCC = 16
VIRT = 768
ROWS = 8
COLS = 32
WIDTH = VIRT // COLS
HALF = VIRT // 2
CHUNK = 256
PARTS = VIRT // CHUNK
KEPT = 9
LOST = 8
F32 = jnp.float32
BF16 = jnp.bfloat16
NT = (((1,), (1,)), ((), ()))
NN = (((1,), (0,)), ((), ()))
HBM = pl.BlockSpec(memory_space=pltpu.HBM)
VMEM = pl.BlockSpec(memory_space=pltpu.VMEM)
SMEM = pl.BlockSpec(memory_space=pltpu.SMEM)


def halves(x):
    high = x.astype(BF16)
    return high, (x - high.astype(F32)).astype(BF16)


def dot3(lh, ll, rh, rl, dims):
    def one(a, b):
        return lax.dot_general(a, b, dims, preferred_element_type=F32)

    return one(lh, rh) + (one(lh, rl) + one(ll, rh))


def transform_kernel(mode_ref, t_ref, a_ref, b_ref, z_ref, t, a, b, z, th, tl, high, low, ins, outs):
    mode = mode_ref[0]
    mine = jnp.where(mode == 0, 1, 0)
    chunks = [slice(i * CHUNK, (i + 1) * CHUNK) for i in range(PARTS)]
    copies = []
    for n, (src, dst) in enumerate(((t_ref, t), (a_ref, a), (b_ref, b))):
        copies.append([pltpu.make_async_copy(src.at[r], dst.at[r], ins.at[n, i]) for i, r in enumerate(chunks)])
        for copy in copies[-1]:
            copy.start()
    for copy, r in zip(copies[0], chunks):
        copy.wait()
        th[r, :], tl[r, :] = halves(t[r, :])
    for copy, r in zip(copies[1], chunks):
        copy.wait()
        ah, al = halves(a[r, :])
        high[mine, r, :], low[mine, r, :] = halves(dot3(ah, al, th[...], tl[...], NN))
    for copy, r in zip(copies[2], chunks):
        copy.wait()
        high[1 - mine, r, :], low[1 - mine, r, :] = halves(b[r, :])
    sends = [pltpu.make_async_copy(z.at[r], z_ref.at[r], outs.at[i]) for i, r in enumerate(chunks)]
    for send, r in zip(sends, chunks):
        z[r, :] = dot3(high[0, r, :], low[0, r, :], high[1], low[1], NT)

        @pl.when(mode != 2)
        def _():
            send.start()

    @pl.when(mode == 2)
    def _():
        tiles = [slice(i * 128, (i + 1) * 128) for i in range(VIRT // 128)]
        for n, i in enumerate(tiles):
            for j in tiles[n:]:
                mean = 0.5 * (z[i, j] + z[j, i].T)
                z[i, j] = mean
                if i != j:
                    z[j, i] = mean.T
        for send in sends:
            send.start()

    for send in sends:
        send.wait()


def transform(mode, t, a, b):
    return pl.pallas_call(
        transform_kernel,
        out_shape=jax.ShapeDtypeStruct((VIRT, VIRT), F32),
        in_specs=[SMEM, HBM, HBM, HBM],
        out_specs=HBM,
        scratch_shapes=[pltpu.VMEM((VIRT, VIRT), F32)] * 4
        + [pltpu.VMEM((VIRT, VIRT), BF16)] * 2
        + [pltpu.VMEM((2, VIRT, VIRT), BF16)] * 2
        + [pltpu.SemaphoreType.DMA((3, PARTS)), pltpu.SemaphoreType.DMA((PARTS,))],
        compiler_params=pltpu.CompilerParams(vmem_limit_bytes=63_500_000),
        name="transform",
    )(mode, t, a, b)


def lost_kernel(row_ref, z_hbm, e_hbm, o_ref, own, other, stage, turned, ins, outs):
    row = row_ref[0]
    loads = []
    for n in range(2 * LOST):
        p0, m = divmod(n, LOST)
        partner = 8 + p0 + m
        there = lax.rem(row + (partner // 2) % ROWS, ROWS)
        loads.append(
            (
                pltpu.make_async_copy(z_hbm.at[p0, there, partner % 2], own.at[n], ins.at[0, n]),
                pltpu.make_async_copy(e_hbm.at[there, partner % 2, p0], other.at[n], ins.at[1, n]),
            )
        )
        for load in loads[-1]:
            load.start()
    for n, pair in enumerate(loads):
        for load in pair:
            load.wait()
        stage[n * WIDTH : (n + 1) * WIDTH, :] = own[n] + other[n]
    sends = []
    for i in range(VIRT // CHUNK):
        rows = slice(i * CHUNK, (i + 1) * CHUNK)
        turned[rows, :] = stage[:, rows].T
        sends.append(pltpu.make_async_copy(turned.at[rows], o_ref.at[rows], outs.at[i]))
        sends[-1].start()
    for send in sends:
        send.wait()


def lost_items(row, z, e):
    return pl.pallas_call(
        lost_kernel,
        out_shape=jax.ShapeDtypeStruct((VIRT, HALF), F32),
        in_specs=[SMEM, HBM, HBM],
        out_specs=HBM,
        scratch_shapes=[
            pltpu.VMEM((2 * LOST, WIDTH, VIRT), F32),
            pltpu.VMEM((2 * LOST, WIDTH, VIRT), F32),
            pltpu.VMEM((HALF, VIRT), F32),
            pltpu.VMEM((VIRT, HALF), F32),
            pltpu.SemaphoreType.DMA((2, 2 * LOST)),
            pltpu.SemaphoreType.DMA((PARTS,)),
        ],
        compiler_params=pltpu.CompilerParams(vmem_limit_bytes=63_500_000),
        name="lost_items",
    )(row, z, e)


def weights(w_ref, row, first, many, tie, count):
    def iota(shape, dim):
        return lax.broadcasted_iota(jnp.int32, shape, dim)

    out = OCC * 8
    pick = (iota((out, OCC), 0) // 8 == iota((out, OCC), 1)).astype(F32)
    m = iota((OCC, many * 8), 1) // 8
    index = (m + (first + 2 * row)) % OCC
    chosen = jnp.where(iota((OCC, many * 8), 0) == index, jnp.where(m == tie, count, 1.0), 0.0)
    full = lax.dot_general(pick, w_ref[...], NT, precision=lax.Precision.HIGHEST, preferred_element_type=F32)
    full = lax.dot_general(full, chosen, NN, precision=lax.Precision.HIGHEST, preferred_element_type=F32)
    same = iota((out, many * 8), 0) % 8 == iota((out, many * 8), 1) % 8
    return halves(jnp.where(same, full, 0.0))


def kept_kernel(row_ref, z_ref, e_ref, w_ref, d_ref, u_ref, r_ref):
    row = row_ref[0]
    count = jnp.where(row < ROWS // 2, 1.0, 0.0)
    for p0 in range(2):
        wh, wl = weights(w_ref, row, p0, KEPT, KEPT - 1, count)
        for g in range(WIDTH // 8):
            rows = slice(g * 8, (g + 1) * 8)
            there = [lax.rem(row + n // 2, ROWS) for n in range(p0, p0 + KEPT)]
            parts = [
                z_ref[p0, t, n % 2, rows, :] + e_ref[t, n % 2, p0, rows, :]
                for t, n in zip(there, range(p0, p0 + KEPT))
            ]
            sh, sl = halves(jnp.concatenate(parts, axis=0))
            total = dot3(wh, wl, sh, sl, NN).reshape(OCC, 8, VIRT)
            scale = 1.0 / d_ref[p0, :, rows, :]
            r_ref[p0, :, rows, :] = scale
            u_ref[p0, :, rows, :] = total * scale


def kept_items(row, z, e, w, d):
    shape = jax.ShapeDtypeStruct(d.shape, F32)
    return pl.pallas_call(
        kept_kernel,
        out_shape=(shape, shape),
        in_specs=[SMEM] + [VMEM] * 4,
        out_specs=(VMEM, VMEM),
        compiler_params=pltpu.CompilerParams(vmem_limit_bytes=40 * 2**20),
        cost_estimate=pl.CostEstimate(flops=2 * 10**9, bytes_accessed=12 * 10**6, transcendentals=0),
        name="kept_items",
    )(row, z, e, w, d)


def finish_kernel(row_ref, back_ref, w_ref, u_hbm, r_hbm, o_ref, tiles, out, u_ref, r_ref, ins, outs):
    row = row_ref[0]
    loads = []
    for p0 in range(2):
        pairs = ((u_hbm, u_ref), (r_hbm, r_ref))
        loads.append([pltpu.make_async_copy(src.at[p0], dst.at[p0], ins.at[n, p0]) for n, (src, dst) in enumerate(pairs)])
    for pair in loads:
        for load in pair:
            load.start()
    group = lax.broadcasted_iota(jnp.int32, (WIDTH, HALF), 1) // WIDTH
    for bit in (1, 2, 4, 8):
        upper = (group // bit) % 2 == 1
        for half in range(2):
            for c in range(16):
                if c & bit:
                    continue
                if bit == 1:
                    low = back_ref[half * 16 + c]
                    high = back_ref[half * 16 + c + bit]
                else:
                    low = tiles[half, c]
                    high = tiles[half, c + bit]
                tiles[half, c] = jnp.where(upper, pltpu.roll(high, bit * WIDTH, 1), low)
                tiles[half, c + bit] = jnp.where(upper, high, pltpu.roll(low, HALF - bit * WIDTH, 1))
    count = jnp.where(row < ROWS // 2, 0.0, 1.0)
    sends = []
    for p0 in range(2):
        wh, wl = weights(w_ref, row, 8 + p0, LOST, 0, count)
        for load in loads[p0]:
            load.wait()
        for g in range(WIDTH // 8):
            rows = slice(g * 8, (g + 1) * 8)
            for half in range(2):
                lanes = slice(half * HALF, (half + 1) * HALF)
                sh, sl = halves(tiles[half, p0 * LOST : (p0 + 1) * LOST, rows, :].reshape(LOST * 8, HALF))
                total = dot3(wh, wl, sh, sl, NN).reshape(OCC, 8, HALF)
                out[p0, :, rows, lanes] = u_ref[p0, :, rows, lanes] + total * r_ref[p0, :, rows, lanes]
            sends.append(pltpu.make_async_copy(out.at[p0, :, rows], o_ref.at[p0, :, rows], outs.at[p0, g]))
            sends[-1].start()
    for send in sends:
        send.wait()


def finish(row, back, w, u, r):
    return pl.pallas_call(
        finish_kernel,
        out_shape=jax.ShapeDtypeStruct(u.shape, F32),
        in_specs=[SMEM, VMEM, VMEM, HBM, HBM],
        out_specs=HBM,
        scratch_shapes=[
            pltpu.VMEM((2, OCC, WIDTH, HALF), F32),
            pltpu.VMEM(u.shape, F32),
            pltpu.VMEM(u.shape, F32),
            pltpu.VMEM(u.shape, F32),
            pltpu.SemaphoreType.DMA((2, 2)),
            pltpu.SemaphoreType.DMA((2, WIDTH // 8)),
        ],
        compiler_params=pltpu.CompilerParams(vmem_limit_bytes=62_500_000),
        name="finish",
    )(row, back, w, u, r)


def on_device(amplitudes, first_rotation, second_rotation, pair_weights, denominators):
    row = lax.axis_index("occi")
    column = lax.axis_index("occj")
    p = 2 * row + column // OCC
    ahead = jnp.mod(column % OCC - p, OCC)
    wins = ((ahead >= 1) & (ahead <= 7)) | ((ahead == 8) & (p < 8))
    mode = jnp.where(ahead == 0, 2, jnp.where(wins, 0, 1)).astype(jnp.int32).reshape(1)
    row_here = row.astype(jnp.int32).reshape(1)

    z = transform(mode, amplitudes[0], first_rotation, second_rotation)
    z = lax.all_to_all(z.reshape(COLS, WIDTH, VIRT), "occj", split_axis=0, concat_axis=0, tiled=True)
    z = z.reshape(2, ROWS, 2, WIDTH, VIRT)
    e = lax.all_to_all(jnp.swapaxes(z, 0, 1), "occi", split_axis=0, concat_axis=0, tiled=True)
    lost = lost_items(row_here, z, e)
    back = lax.all_to_all(lost.reshape(COLS, WIDTH, HALF), "occj", split_axis=0, concat_axis=0, tiled=True)
    u, r = kept_items(row_here, z, e, pair_weights, denominators)
    return finish(row_here, back, pair_weights, u, r)


def solution(mesh):
    placed = (P(("occi", "occj"), None, None), P(), P(), P(), P("occi", None, "occj", None))
    return jax.shard_map(
        on_device,
        mesh=mesh,
        in_specs=placed,
        out_specs=P("occi", None, "occj", None),
        check_vma=False,
    )
```

time: 209 us -> 166 us (0.79)
  blocking collectives: 0 us -> 104 us
  waiting for transfers between devices: 121 us -> 23.1 us
  matrix products: 28 us -> 0 us
  starting transfers between devices: 32.6 us -> 6.64 us
  Pallas kernels: 0 us -> 23.5 us
  local copies, waits for them, and re-layouts: 26.9 us -> 7.55 us
    all_to_all x0 -> x2, blocking collectives: none -> 104 us  [the longest x1 69.9 us: on_device(): lax.all_to_all(z.reshape(COLS, WIDTH, VIRT), 'occj', split_axis=0, concat...]
    all_to_all x3 -> x1, waiting for transfers between devices: 121 us -> 23.1 us  [on_device(): lax.all_to_all(lost.reshape(COLS, WIDTH, HALF), 'occj', split_axis=0, con...]
    dot_general x3 -> x0, matrix products: 28 us -> none  [the longest x1 12.9 us: on_device(): jnp.einsum('ac,pcd->pad', first_rotation, amplitudes, precision=highest)]
    all_to_all x3 -> x1, starting transfers between devices: 32.6 us -> 6.64 us  [on_device(): lax.all_to_all(lost.reshape(COLS, WIDTH, HALF), 'occj', split_axis=0, con...]
    pallas_call x0 -> x4, Pallas kernels: none -> 23.5 us  [the longest x1 13 us: transform(): pl.pallas_call(transform_kernel, out_shape=jax.ShapeDtypeStruct((VIRT, VI...]
    transpose x1 -> x0, local copies, waits for them, and re-layouts: 6.72 us -> none  [on_device(): outgoing = (jnp.swapaxes(finished, 1, 2), finished)]
    dot_general x1 -> x0, local copies, waits for them, and re-layouts: 3.83 us -> none  [on_device(): jnp.einsum('pad,bd->pab', halfway, second_rotation, precision=highest)]
    div x1 -> x0, local copies, waits for them, and re-layouts: 2.77 us -> none  [on_device(): return contracted / denominators]
  transfers between devices with their start and end apart: 3 -> 1, of which waited for: 3 -> 1; matrix products, arithmetic and copies ran while one was open for 6% -> 0% of each run, Pallas kernels for 0% -> 1%
where the time goes in v2:
time: 166 us; the launch traced here: 165 us
  blocking collectives  104 us (63%)
  Pallas kernels  23.5 us (14%)
  waiting for transfers between devices  23.1 us (14%)
  local copies, waits for them, and re-layouts  7.55 us (5%)
  starting transfers between devices  6.64 us (4%)
    all_to_all x1, blocking collectives, on_device(): lax.all_to_all(z.reshape(COLS, WIDTH, VIRT), 'occj', split_axis=0, concat...  69.9 us
    all_to_all x1, blocking collectives, on_device(): lax.all_to_all(jnp.swapaxes(z, 0, 1), 'occi', split_axis=0, concat_axis=0...  34.3 us
    all_to_all x1, waiting for transfers between devices, on_device(): lax.all_to_all(lost.reshape(COLS, WIDTH, HALF), 'occj', split_axis=0, con...  23.1 us
    pallas_call x1, Pallas kernels, transform(): pl.pallas_call(transform_kernel, out_shape=jax.ShapeDtypeStruct((VIRT, VI...  13 us
    unnamed x14, local copies, waits for them, and re-layouts  7.35 us
    all_to_all x1, starting transfers between devices, on_device(): lax.all_to_all(lost.reshape(COLS, WIDTH, HALF), 'occj', split_axis=0, con...  6.64 us
    pallas_call x1, Pallas kernels, finish(): pl.pallas_call(finish_kernel, out_shape=jax.ShapeDtypeStruct(u.shape, F32...  5.27 us
  transfers between devices with their start and end apart: 1, of which 1 were waited for; matrix products, arithmetic and copies ran while one was open for 0% of the time, Pallas kernels for 1%

profile of v2, /device:TPU:1, one launch (start us, length us, event | category | flops | bytes accessed | tf_op | source)
XLA Modules:
  0.0 165.1 jit_solution(3193025586911709760)
XLA Ops:
  0.0 13.0 %transform.1 = f32[768,768]{1,0:T(8,128)} custom-call(s32[1]{0:T(128)} %bitcast.1.mode_ref, f32[768,768]{1,0:T(8,128)} %bitcast.15, f32[768,768]{1,0:T(8,128)} %a_ref.1, f32[768,768]{1,0:T(8,128)} %b_ref.1), custom_call_target="tpu_custom_call" | custom-call | tf_op jit(solution)/shard_map/transform/pallas_call | solution.py:83
  13.0 69.9 %all_to_all.15 = f32[32,24,768]{2,1,0:T(8,128)S(1)} all-to-all(f32[32,24,768]{2,1,0:T(8,128)} %bitcast.13), channel_id=1, replica_groups=mesh['occi'=8,'occj'=32] {'occj'}, dimensions={0} | all-to-all | bytes 4718592 | tf_op jit(solution)/shard_map/all_to_all | solution.py:264
  82.8 0.0 copy-start
  82.8 0.2 copy.10
  83.0 1.2 copy-done
  84.2 34.3 %all_to_all.16.e_hbm.e_ref = f32[8,2,2,24,768]{4,3,2,1,0:T(8,128)} all-to-all(f32[8,2,2,24,768]{4,3,2,1,0:T(8,128)S(1)} %bitcast.12), channel_id=1, replica_groups=mesh['occi'=8,'occj'=32] {'occi'}, dimensions={0} | all-to-all | bytes 4718592 | tf_op jit(solution)/shard_map/all_to_all | solution.py:266
  118.5 0.0 copy-start.5
  118.5 3.2 %lost_items.1 = f32[768,384]{1,0:T(8,128)} custom-call(s32[1]{0:T(128)} %bitcast.row_ref, f32[2,8,2,24,768]{4,3,2,1,0:T(8,128)} %bitcast.10, f32[8,2,2,24,768]{4,3,2,1,0:T(8,128)} %all_to_all.16.e_hbm.e_ref), custom_call_target="tpu_custom_call" | custom-call | tf_op jit(solution)/shard_map/lost_items/pallas_call | solution.py:127
  121.7 0.0 copy-start.1
  121.7 6.6 %all-to-all-start.2 = ((f32[32,24,384]{2,1,0:T(8,128)}), f32[32,24,384]{2,1,0:T(8,128)}, u32[]{:S(2)}, u32[]{:S(2)}) async-start(f32[32,24,384]{2,1,0:T(8,128)} %bitcast.14), calls=%async_computation.2 | async-start | bytes 2359296 | tf_op jit(solution)/shard_map/all_to_all | solution.py:268
  128.4 0.0 copy-done.5
  128.4 0.0 copy-done.1
  128.4 0.0 copy-start.2
  128.4 1.7 %copy-done.2 = f32[8,2,2,24,768]{4,3,2,1,0:T(8,128)S(1)} copy-done((f32[8,2,2,24,768]{4,3,2,1,0:T(8,128)S(1)}, f32[8,2,2,24,768]{4,3,2,1,0:T(8,128)}, u32[]{:S(2)}) %copy-start.2) | copy-done | bytes 2359320
  130.1 0.0 copy-start.6
  130.1 1.7 %copy-done.6 = f32[2,16,24,768]{3,2,1,0:T(8,128)S(1)} copy-done((f32[2,16,24,768]{3,2,1,0:T(8,128)S(1)}, f32[2,16,24,768]{3,2,1,0:T(8,128)}, u32[]{:S(2)}) %copy-start.6) | copy-done | bytes 2359320
  131.7 2.0 %kept_items.1 = (f32[2,16,24,768]{3,2,1,0:T(8,128)S(1)}, f32[2,16,24,768]{3,2,1,0:T(8,128)S(1)}) custom-call(s32[1]{0:T(128)} %bitcast.row_ref, f32[2,8,2,24,768]{4,3,2,1,0:T(8,128)S(1)} %bitcast.11, f32[8,2,2,24,768]{4,3,2,1,0:T(8,128)S(1)} %copy-done.2, f32[16,16]{1,0:T(8,128)S(1)} %copy-done.5, f32[2,16,24,768]{3,2,1,0:T(8,128)S(1)} %copy-done.6), custom_call_target="tpu_custom_call" | custom-call | flops 2000000000 | bytes 12000000 | tf_op jit(solution)/shard_map/kept_items/pallas_call | solution.py:181
  133.8 0.0 copy-start.3
  133.8 1.4 copy-done.3
  135.2 0.0 copy-start.4
  135.2 1.4 copy-done.4
  136.6 23.1 %all-to-all-done.2.back_ref = f32[32,24,384]{2,1,0:T(8,128)} async-done(((f32[32,24,384]{2,1,0:T(8,128)}), f32[32,24,384]{2,1,0:T(8,128)}, u32[]{:S(2)}, u32[]{:S(2)}) %all-to-all-start.2) | async-done | bytes 1179680 | tf_op jit(solution)/shard_map/all_to_all | solution.py:268
  159.7 5.3 %finish.1 = f32[2,16,24,768]{3,2,1,0:T(8,128)} custom-call(s32[1]{0:T(128)} %bitcast.row_ref, f32[32,24,384]{2,1,0:T(8,128)} %all-to-all-done.2.back_ref, f32[16,16]{1,0:T(8,128)} %w_ref.3, f32[2,16,24,768]{3,2,1,0:T(8,128)} %copy-done.3, f32[2,16,24,768]{3,2,1,0:T(8,128)} %copy-done.4), custom_call_target="tpu_custom_call" | custom-call | tf_op jit(solution)/shard_map/finish/pallas_call | solution.py:236
Async XLA Ops:
  82.8 1.4 copy-start
  118.5 9.9 %copy-start.5 = (f32[16,16]{1,0:T(8,128)S(1)}, f32[16,16]{1,0:T(8,128)}, u32[]{:S(2)}) copy-start(f32[16,16]{1,0:T(8,128)} %w_ref.3) | copy-start | bytes 3076
  121.7 6.7 %copy-start.1 = (f32[32,24,768]{2,1,0:T(8,128)S(1)}, f32[32,24,768]{2,1,0:T(8,128)}, u32[]{:S(2)}) copy-start(f32[32,24,768]{2,1,0:T(8,128)} %copy-done) | copy-start | bytes 7077892
  121.7 38.0 %all-to-all-start.2 = ((f32[32,24,384]{2,1,0:T(8,128)}), f32[32,24,384]{2,1,0:T(8,128)}, u32[]{:S(2)}, u32[]{:S(2)}) async-start(f32[32,24,384]{2,1,0:T(8,128)} %bitcast.14), calls=%async_computation.2 | async-start | bytes 2359296 | tf_op jit(solution)/shard_map/all_to_all | solution.py:268
  128.4 1.7 %copy-start.2 = (f32[8,2,2,24,768]{4,3,2,1,0:T(8,128)S(1)}, f32[8,2,2,24,768]{4,3,2,1,0:T(8,128)}, u32[]{:S(2)}) copy-start(f32[8,2,2,24,768]{4,3,2,1,0:T(8,128)} %all_to_all.16.e_hbm.e_ref) | copy-start | bytes 7077892
  130.1 1.7 %copy-start.6 = (f32[2,16,24,768]{3,2,1,0:T(8,128)S(1)}, f32[2,16,24,768]{3,2,1,0:T(8,128)}, u32[]{:S(2)}) copy-start(f32[2,16,24,768]{3,2,1,0:T(8,128)} %d_ref.1) | copy-start | bytes 7077892
  133.8 1.4 copy-start.3
  135.2 1.4 copy-start.4

commit v3 on v2

--- a/solution.py
+++ b/solution.py
@@ -36,28 +36,42 @@
     return one(lh, rh) + (one(lh, rl) + one(ll, rh))
 
 
-def transform_kernel(mode_ref, t_ref, a_ref, b_ref, z_ref, t, a, b, z, th, tl, high, low, ins, outs):
+def transform_kernel(mode_ref, t_ref, a_ref, b_ref, z_ref, t, a, b, z, t3, a3, pair, ins, outs):
     mode = mode_ref[0]
     mine = jnp.where(mode == 0, 1, 0)
     chunks = [slice(i * CHUNK, (i + 1) * CHUNK) for i in range(PARTS)]
-    copies = []
+    thirds = [slice(i * VIRT, (i + 1) * VIRT) for i in range(3)]
+    loads = []
     for n, (src, dst) in enumerate(((t_ref, t), (a_ref, a), (b_ref, b))):
-        copies.append([pltpu.make_async_copy(src.at[r], dst.at[r], ins.at[n, i]) for i, r in enumerate(chunks)])
-        for copy in copies[-1]:
-            copy.start()
-    for copy, r in zip(copies[0], chunks):
-        copy.wait()
-        th[r, :], tl[r, :] = halves(t[r, :])
-    for copy, r in zip(copies[1], chunks):
-        copy.wait()
-        ah, al = halves(a[r, :])
-        high[mine, r, :], low[mine, r, :] = halves(dot3(ah, al, th[...], tl[...], NN))
-    for copy, r in zip(copies[2], chunks):
-        copy.wait()
-        high[1 - mine, r, :], low[1 - mine, r, :] = halves(b[r, :])
+        loads.append([pltpu.make_async_copy(src.at[r], dst.at[r], ins.at[n, i]) for i, r in enumerate(chunks)])
+    for load in loads[0] + loads[1]:
+        load.start()
+
+    def put(slot, rows, x, right):
+        h, l = halves(x)
+        pair[slot, rows, thirds[0]] = h
+        pair[slot, rows, thirds[1]] = jnp.where(right, l, h)
+        pair[slot, rows, thirds[2]] = jnp.where(right, h, l)
+
+    for i, (load, r) in enumerate(zip(loads[0], chunks)):
+        load.wait()
+        h, l = halves(t[r, :])
+        for n, x in enumerate((h, l, h)):
+            t3[n * VIRT + i * CHUNK : n * VIRT + (i + 1) * CHUNK, :] = x
+    for load in loads[2]:
+        load.start()
+    for load, r in zip(loads[1], chunks):
+        load.wait()
+        h, l = halves(a[r, :])
+        for third, x in zip(thirds, (h, h, l)):
+            a3[r, third] = x
+        put(mine, r, lax.dot_general(a3[r, :], t3[...], NN, preferred_element_type=F32), mode == 0)
+    for load, r in zip(loads[2], chunks):
+        load.wait()
+        put(1 - mine, r, b[r, :], mode != 0)
     sends = [pltpu.make_async_copy(z.at[r], z_ref.at[r], outs.at[i]) for i, r in enumerate(chunks)]
     for send, r in zip(sends, chunks):
-        z[r, :] = dot3(high[0, r, :], low[0, r, :], high[1], low[1], NT)
+        z[r, :] = lax.dot_general(pair[0, r, :], pair[1], NT, preferred_element_type=F32)
 
         @pl.when(mode != 2)
         def _():
@@ -86,35 +100,42 @@
         in_specs=[SMEM, HBM, HBM, HBM],
         out_specs=HBM,
         scratch_shapes=[pltpu.VMEM((VIRT, VIRT), F32)] * 4
-        + [pltpu.VMEM((VIRT, VIRT), BF16)] * 2
-        + [pltpu.VMEM((2, VIRT, VIRT), BF16)] * 2
+        + [pltpu.VMEM((3 * VIRT, VIRT), BF16), pltpu.VMEM((VIRT, 3 * VIRT), BF16), pltpu.VMEM((2, VIRT, 3 * VIRT), BF16)]
         + [pltpu.SemaphoreType.DMA((3, PARTS)), pltpu.SemaphoreType.DMA((PARTS,))],
         compiler_params=pltpu.CompilerParams(vmem_limit_bytes=63_500_000),
         name="transform",
     )(mode, t, a, b)
 
 
+STEPS = (4, 5, 6, 7, 0)
+
+
 def lost_kernel(row_ref, z_hbm, e_hbm, o_ref, own, other, stage, turned, ins, outs):
     row = row_ref[0]
     loads = []
-    for n in range(2 * LOST):
-        p0, m = divmod(n, LOST)
-        partner = 8 + p0 + m
-        there = lax.rem(row + (partner // 2) % ROWS, ROWS)
+    for i, step in enumerate(STEPS[:4]):
+        there = lax.rem(row + step, ROWS)
         loads.append(
-            (
-                pltpu.make_async_copy(z_hbm.at[p0, there, partner % 2], own.at[n], ins.at[0, n]),
-                pltpu.make_async_copy(e_hbm.at[there, partner % 2, p0], other.at[n], ins.at[1, n]),
-            )
+            [pltpu.make_async_copy(z_hbm.at[p0, there], own.at[p0, i], ins.at[i, p0]) for p0 in range(2)]
+            + [pltpu.make_async_copy(e_hbm.at[there], other.at[i], ins.at[i, 2])]
         )
-        for load in loads[-1]:
+    loads.append([pltpu.make_async_copy(z_hbm.at[p0, row, 1 - p0], own.at[p0, 4, 1 - p0], ins.at[4, p0]) for p0 in range(2)])
+    for group in loads:
+        for load in group:
             load.start()
-    for n, pair in enumerate(loads):
-        for load in pair:
+    for i, group in enumerate(loads):
+        for load in group:
             load.wait()
-        stage[n * WIDTH : (n + 1) * WIDTH, :] = own[n] + other[n]
+        for p0 in range(2):
+            for m in range(LOST):
+                partner = 8 + p0 + m
+                if (partner // 2) % ROWS == STEPS[i]:
+                    q0 = partner % 2
+                    second = own[1 - p0, i, p0] if i == 4 else other[i, q0, p0]
+                    at = (p0 * LOST + m) * WIDTH
+                    stage[at : at + WIDTH, :] = own[p0, i, q0] + second
     sends = []
-    for i in range(VIRT // CHUNK):
+    for i in range(PARTS):
         rows = slice(i * CHUNK, (i + 1) * CHUNK)
         turned[rows, :] = stage[:, rows].T
         sends.append(pltpu.make_async_copy(turned.at[rows], o_ref.at[rows], outs.at[i]))
@@ -130,11 +151,11 @@
         in_specs=[SMEM, HBM, HBM],
         out_specs=HBM,
         scratch_shapes=[
-            pltpu.VMEM((2 * LOST, WIDTH, VIRT), F32),
-            pltpu.VMEM((2 * LOST, WIDTH, VIRT), F32),
+            pltpu.VMEM((2, 5, 2, WIDTH, VIRT), F32),
+            pltpu.VMEM((4, 2, 2, WIDTH, VIRT), F32),
             pltpu.VMEM((HALF, VIRT), F32),
             pltpu.VMEM((VIRT, HALF), F32),
-            pltpu.SemaphoreType.DMA((2, 2 * LOST)),
+            pltpu.SemaphoreType.DMA((5, 3)),
             pltpu.SemaphoreType.DMA((PARTS,)),
         ],
         compiler_params=pltpu.CompilerParams(vmem_limit_bytes=63_500_000),
@@ -189,45 +210,50 @@
     )(row, z, e, w, d)
 
 
-def finish_kernel(row_ref, back_ref, w_ref, u_hbm, r_hbm, o_ref, tiles, out, u_ref, r_ref, ins, outs):
+def finish_kernel(row_ref, back_hbm, w_ref, u_hbm, r_hbm, o_ref, back, u, r, out, ins, outs):
     row = row_ref[0]
+    groups = [slice(g * 8, (g + 1) * 8) for g in range(WIDTH // 8)]
     loads = []
-    for p0 in range(2):
-        pairs = ((u_hbm, u_ref), (r_hbm, r_ref))
-        loads.append([pltpu.make_async_copy(src.at[p0], dst.at[p0], ins.at[n, p0]) for n, (src, dst) in enumerate(pairs)])
-    for pair in loads:
-        for load in pair:
+    for g, rows in enumerate(groups):
+        loads.append(
+            [
+                pltpu.make_async_copy(back_hbm.at[:, rows], back.at[:, rows], ins.at[0, g]),
+                pltpu.make_async_copy(u_hbm.at[:, :, rows], u.at[:, :, rows], ins.at[1, g]),
+                pltpu.make_async_copy(r_hbm.at[:, :, rows], r.at[:, :, rows], ins.at[2, g]),
+            ]
+        )
+        for load in loads[-1]:
             load.start()
-    group = lax.broadcasted_iota(jnp.int32, (WIDTH, HALF), 1) // WIDTH
-    for bit in (1, 2, 4, 8):
-        upper = (group // bit) % 2 == 1
-        for half in range(2):
-            for c in range(16):
-                if c & bit:
-                    continue
-                if bit == 1:
-                    low = back_ref[half * 16 + c]
-                    high = back_ref[half * 16 + c + bit]
-                else:
-                    low = tiles[half, c]
-                    high = tiles[half, c + bit]
-                tiles[half, c] = jnp.where(upper, pltpu.roll(high, bit * WIDTH, 1), low)
-                tiles[half, c + bit] = jnp.where(upper, high, pltpu.roll(low, HALF - bit * WIDTH, 1))
     count = jnp.where(row < ROWS // 2, 0.0, 1.0)
-    sends = []
+    spread = []
     for p0 in range(2):
         wh, wl = weights(w_ref, row, 8 + p0, LOST, 0, count)
-        for load in loads[p0]:
-            load.wait()
-        for g in range(WIDTH // 8):
-            rows = slice(g * 8, (g + 1) * 8)
-            for half in range(2):
-                lanes = slice(half * HALF, (half + 1) * HALF)
-                sh, sl = halves(tiles[half, p0 * LOST : (p0 + 1) * LOST, rows, :].reshape(LOST * 8, HALF))
-                total = dot3(wh, wl, sh, sl, NN).reshape(OCC, 8, HALF)
-                out[p0, :, rows, lanes] = u_ref[p0, :, rows, lanes] + total * r_ref[p0, :, rows, lanes]
-            sends.append(pltpu.make_async_copy(out.at[p0, :, rows], o_ref.at[p0, :, rows], outs.at[p0, g]))
-            sends[-1].start()
+        spread.append(jnp.concatenate([wh, wh, wl], axis=1))
+    group = lax.broadcasted_iota(jnp.int32, (8, HALF), 1) // WIDTH
+    sends = []
+    for g, rows in enumerate(groups):
+        loads[g][0].wait()
+        for half in range(2):
+            lanes = slice(half * HALF, (half + 1) * HALF)
+            x = [back[half * 16 + c, rows, :] for c in range(16)]
+            for bit in (1, 2, 4, 8):
+                upper = (group // bit) % 2 == 1
+                for c in range(16):
+                    if not c & bit:
+                        low, high = x[c], x[c + bit]
+                        x[c] = jnp.where(upper, pltpu.roll(high, bit * WIDTH, 1), low)
+                        x[c + bit] = jnp.where(upper, high, pltpu.roll(low, HALF - bit * WIDTH, 1))
+            if half == 0:
+                for load in loads[g][1:]:
+                    load.wait()
+            for p0 in range(2):
+                sh, sl = halves(jnp.concatenate(x[p0 * LOST : (p0 + 1) * LOST], axis=0))
+                stacked = jnp.concatenate([sh, sl, sh], axis=0)
+                total = lax.dot_general(spread[p0], stacked, NN, preferred_element_type=F32)
+                total = total.reshape(OCC, 8, HALF)
+                out[p0, :, rows, lanes] = u[p0, :, rows, lanes] + total * r[p0, :, rows, lanes]
+        sends.append(pltpu.make_async_copy(out.at[:, :, rows], o_ref.at[:, :, rows], outs.at[g]))
+        sends[-1].start()
     for send in sends:
         send.wait()
 
@@ -236,16 +262,11 @@
     return pl.pallas_call(
         finish_kernel,
         out_shape=jax.ShapeDtypeStruct(u.shape, F32),
-        in_specs=[SMEM, VMEM, VMEM, HBM, HBM],
+        in_specs=[SMEM, HBM, VMEM, HBM, HBM],
         out_specs=HBM,
-        scratch_shapes=[
-            pltpu.VMEM((2, OCC, WIDTH, HALF), F32),
-            pltpu.VMEM(u.shape, F32),
-            pltpu.VMEM(u.shape, F32),
-            pltpu.VMEM(u.shape, F32),
-            pltpu.SemaphoreType.DMA((2, 2)),
-            pltpu.SemaphoreType.DMA((2, WIDTH // 8)),
-        ],
+        scratch_shapes=[pltpu.VMEM(back.shape, F32)]
+        + [pltpu.VMEM(u.shape, F32)] * 3
+        + [pltpu.SemaphoreType.DMA((3, WIDTH // 8)), pltpu.SemaphoreType.DMA((WIDTH // 8,))],
         compiler_params=pltpu.CompilerParams(vmem_limit_bytes=62_500_000),
         name="finish",
     )(row, back, w, u, r)

time: 166 us -> 163 us (0.982)
  Pallas kernels: 23.5 us -> 21.3 us
    pallas_call x1, Pallas kernels: 13 us -> 10.6 us  [transform(): pl.pallas_call(transform_kernel, out_shape=jax.ShapeDtypeStruct((VIRT, VI...]
where the time goes in v3:
time: 163 us
  blocking collectives  104 us (64%)
  waiting for transfers between devices  23.1 us (14%)
  Pallas kernels  21.3 us (13%)
  local copies, waits for them, and re-layouts  7.55 us (5%)
  starting transfers between devices  6.64 us (4%)
    all_to_all x1, blocking collectives, on_device(): lax.all_to_all(z.reshape(COLS, WIDTH, VIRT), 'occj', split_axis=0, concat...  70.9 us
    all_to_all x1, blocking collectives, on_device(): lax.all_to_all(jnp.swapaxes(z, 0, 1), 'occi', split_axis=0, concat_axis=0...  33.2 us
    all_to_all x1, waiting for transfers between devices, on_device(): lax.all_to_all(lost.reshape(COLS, WIDTH, HALF), 'occj', split_axis=0, con...  23.1 us
    pallas_call x1, Pallas kernels, transform(): pl.pallas_call(transform_kernel, out_shape=jax.ShapeDtypeStruct((VIRT, VI...  10.6 us
    unnamed x14, local copies, waits for them, and re-layouts  7.35 us
    all_to_all x1, starting transfers between devices, on_device(): lax.all_to_all(lost.reshape(COLS, WIDTH, HALF), 'occj', split_axis=0, con...  6.64 us
    pallas_call x1, Pallas kernels, finish(): pl.pallas_call(finish_kernel, out_shape=jax.ShapeDtypeStruct(u.shape, F32...  5.59 us
  transfers between devices with their start and end apart: 1, of which 1 were waited for; matrix products, arithmetic and copies ran while one was open for 0% of the time, Pallas kernels for 1%

profile of v3, /device:TPU:1, one launch (start us, length us, event | category | flops | bytes accessed | tf_op | source)
XLA Modules:
  0.0 163.0 jit_solution(2326722274473143873)
XLA Ops:
  0.0 10.6 %transform.1 = f32[768,768]{1,0:T(8,128)} custom-call(s32[1]{0:T(128)} %bitcast.1.mode_ref, f32[768,768]{1,0:T(8,128)} %bitcast.15, f32[768,768]{1,0:T(8,128)} %a_ref.1, f32[768,768]{1,0:T(8,128)} %b_ref.1), custom_call_target="tpu_custom_call" | custom-call | tf_op jit(solution)/shard_map/transform/pallas_call | solution.py:97
  10.7 70.9 %all_to_all.15 = f32[32,24,768]{2,1,0:T(8,128)S(1)} all-to-all(f32[32,24,768]{2,1,0:T(8,128)} %bitcast.13), channel_id=1, replica_groups=mesh['occi'=8,'occj'=32] {'occj'}, dimensions={0} | all-to-all | bytes 4718592 | tf_op jit(solution)/shard_map/all_to_all | solution.py:285
  81.6 0.0 copy-start
  81.6 0.2 copy.10
  81.8 1.2 copy-done
  83.0 33.2 %all_to_all.16.e_hbm.e_ref = f32[8,2,2,24,768]{4,3,2,1,0:T(8,128)} all-to-all(f32[8,2,2,24,768]{4,3,2,1,0:T(8,128)S(1)} %bitcast.12), channel_id=1, replica_groups=mesh['occi'=8,'occj'=32] {'occi'}, dimensions={0} | all-to-all | bytes 4718592 | tf_op jit(solution)/shard_map/all_to_all | solution.py:287
  116.2 0.0 copy-start.5
  116.2 3.1 %lost_items.1 = f32[768,384]{1,0:T(8,128)} custom-call(s32[1]{0:T(128)} %bitcast.row_ref, f32[2,8,2,24,768]{4,3,2,1,0:T(8,128)} %bitcast.10, f32[8,2,2,24,768]{4,3,2,1,0:T(8,128)} %all_to_all.16.e_hbm.e_ref), custom_call_target="tpu_custom_call" | custom-call | tf_op jit(solution)/shard_map/lost_items/pallas_call | solution.py:148
  119.3 0.0 copy-start.1
  119.3 6.6 %all-to-all-start.2 = ((f32[32,24,384]{2,1,0:T(8,128)}), f32[32,24,384]{2,1,0:T(8,128)}, u32[]{:S(2)}, u32[]{:S(2)}) async-start(f32[32,24,384]{2,1,0:T(8,128)} %bitcast.14), calls=%async_computation.2 | async-start | bytes 2359296 | tf_op jit(solution)/shard_map/all_to_all | solution.py:289
  125.9 0.0 copy-done.5
  125.9 0.0 copy-done.1
  125.9 0.0 copy-start.2
  125.9 1.7 %copy-done.2 = f32[8,2,2,24,768]{4,3,2,1,0:T(8,128)S(1)} copy-done((f32[8,2,2,24,768]{4,3,2,1,0:T(8,128)S(1)}, f32[8,2,2,24,768]{4,3,2,1,0:T(8,128)}, u32[]{:S(2)}) %copy-start.2) | copy-done | bytes 2359320
  127.6 0.0 copy-start.6
  127.6 1.7 %copy-done.6 = f32[2,16,24,768]{3,2,1,0:T(8,128)S(1)} copy-done((f32[2,16,24,768]{3,2,1,0:T(8,128)S(1)}, f32[2,16,24,768]{3,2,1,0:T(8,128)}, u32[]{:S(2)}) %copy-start.6) | copy-done | bytes 2359320
  129.3 2.0 %kept_items.1 = (f32[2,16,24,768]{3,2,1,0:T(8,128)S(1)}, f32[2,16,24,768]{3,2,1,0:T(8,128)S(1)}) custom-call(s32[1]{0:T(128)} %bitcast.row_ref, f32[2,8,2,24,768]{4,3,2,1,0:T(8,128)S(1)} %bitcast.11, f32[8,2,2,24,768]{4,3,2,1,0:T(8,128)S(1)} %copy-done.2, f32[16,16]{1,0:T(8,128)S(1)} %copy-done.5, f32[2,16,24,768]{3,2,1,0:T(8,128)S(1)} %copy-done.6), custom_call_target="tpu_custom_call" | custom-call | flops 2000000000 | bytes 12000000 | tf_op jit(solution)/shard_map/kept_items/pallas_call | solution.py:202
  131.3 0.0 copy-start.3
  131.3 1.4 copy-done.3
  132.7 0.0 copy-start.4
  132.7 1.4 copy-done.4
  134.1 23.1 %all-to-all-done.2.back_hbm = f32[32,24,384]{2,1,0:T(8,128)} async-done(((f32[32,24,384]{2,1,0:T(8,128)}), f32[32,24,384]{2,1,0:T(8,128)}, u32[]{:S(2)}, u32[]{:S(2)}) %all-to-all-start.2) | async-done | bytes 1179680 | tf_op jit(solution)/shard_map/all_to_all | solution.py:289
  157.2 5.6 %finish.1 = f32[2,16,24,768]{3,2,1,0:T(8,128)} custom-call(s32[1]{0:T(128)} %bitcast.row_ref, f32[32,24,384]{2,1,0:T(8,128)} %all-to-all-done.2.back_hbm, f32[16,16]{1,0:T(8,128)} %w_ref.3, f32[2,16,24,768]{3,2,1,0:T(8,128)} %copy-done.3, f32[2,16,24,768]{3,2,1,0:T(8,128)} %copy-done.4), custom_call_target="tpu_custom_call" | custom-call | tf_op jit(solution)/shard_map/finish/pallas_call | solution.py:262
Async XLA Ops:
  81.6 1.4 copy-start
  116.2 9.7 %copy-start.5 = (f32[16,16]{1,0:T(8,128)S(1)}, f32[16,16]{1,0:T(8,128)}, u32[]{:S(2)}) copy-start(f32[16,16]{1,0:T(8,128)} %w_ref.3) | copy-start | bytes 3076
  119.3 6.7 %copy-start.1 = (f32[32,24,768]{2,1,0:T(8,128)S(1)}, f32[32,24,768]{2,1,0:T(8,128)}, u32[]{:S(2)}) copy-start(f32[32,24,768]{2,1,0:T(8,128)} %copy-done) | copy-start | bytes 7077892
  119.3 38.0 %all-to-all-start.2 = ((f32[32,24,384]{2,1,0:T(8,128)}), f32[32,24,384]{2,1,0:T(8,128)}, u32[]{:S(2)}, u32[]{:S(2)}) async-start(f32[32,24,384]{2,1,0:T(8,128)} %bitcast.14), calls=%async_computation.2 | async-start | bytes 2359296 | tf_op jit(solution)/shard_map/all_to_all | solution.py:289
  125.9 1.7 %copy-start.2 = (f32[8,2,2,24,768]{4,3,2,1,0:T(8,128)S(1)}, f32[8,2,2,24,768]{4,3,2,1,0:T(8,128)}, u32[]{:S(2)}) copy-start(f32[8,2,2,24,768]{4,3,2,1,0:T(8,128)} %all_to_all.16.e_hbm.e_ref) | copy-start | bytes 7077892
  127.6 1.7 %copy-start.6 = (f32[2,16,24,768]{3,2,1,0:T(8,128)S(1)}, f32[2,16,24,768]{3,2,1,0:T(8,128)}, u32[]{:S(2)}) copy-start(f32[2,16,24,768]{3,2,1,0:T(8,128)} %d_ref.1) | copy-start | bytes 7077892
  131.3 1.4 copy-start.3
  132.7 1.4 copy-start.4

commit v4 on v3

--- a/solution.py
+++ b/solution.py
@@ -107,17 +107,17 @@
     )(mode, t, a, b)
 
 
-STEPS = (4, 5, 6, 7, 0)
-
-
-def lost_kernel(row_ref, z_hbm, e_hbm, o_ref, own, other, stage, turned, ins, outs):
+STEPS = (7, 6, 5, 4, 0)
+
+
+def lost_kernel(row_ref, z_hbm, g7, g6, g5, g4, o_ref, own, other, stage, turned, ins, outs):
     row = row_ref[0]
     loads = []
-    for i, step in enumerate(STEPS[:4]):
+    for i, (step, got) in enumerate(zip(STEPS, (g7, g6, g5, g4))):
         there = lax.rem(row + step, ROWS)
         loads.append(
             [pltpu.make_async_copy(z_hbm.at[p0, there], own.at[p0, i], ins.at[i, p0]) for p0 in range(2)]
-            + [pltpu.make_async_copy(e_hbm.at[there], other.at[i], ins.at[i, 2])]
+            + [pltpu.make_async_copy(got, other.at[i], ins.at[i, 2])]
         )
     loads.append([pltpu.make_async_copy(z_hbm.at[p0, row, 1 - p0], own.at[p0, 4, 1 - p0], ins.at[4, p0]) for p0 in range(2)])
     for group in loads:
@@ -144,11 +144,11 @@
         send.wait()
 
 
-def lost_items(row, z, e):
+def lost_items(row, z, *got):
     return pl.pallas_call(
         lost_kernel,
         out_shape=jax.ShapeDtypeStruct((VIRT, HALF), F32),
-        in_specs=[SMEM, HBM, HBM],
+        in_specs=[SMEM] + [HBM] * 5,
         out_specs=HBM,
         scratch_shapes=[
             pltpu.VMEM((2, 5, 2, WIDTH, VIRT), F32),
@@ -160,7 +160,7 @@
         ],
         compiler_params=pltpu.CompilerParams(vmem_limit_bytes=63_500_000),
         name="lost_items",
-    )(row, z, e)
+    )(row, z, *got)
 
 
 def weights(w_ref, row, first, many, tie, count):
@@ -178,18 +178,20 @@
     return halves(jnp.where(same, full, 0.0))
 
 
-def kept_kernel(row_ref, z_ref, e_ref, w_ref, d_ref, u_ref, r_ref):
+def kept_kernel(row_ref, z_ref, g4, g3, g2, g1, w_ref, d_ref, u_ref, r_ref):
     row = row_ref[0]
+    got = {4: g4, 3: g3, 2: g2, 1: g1}
     count = jnp.where(row < ROWS // 2, 1.0, 0.0)
     for p0 in range(2):
         wh, wl = weights(w_ref, row, p0, KEPT, KEPT - 1, count)
         for g in range(WIDTH // 8):
             rows = slice(g * 8, (g + 1) * 8)
-            there = [lax.rem(row + n // 2, ROWS) for n in range(p0, p0 + KEPT)]
-            parts = [
-                z_ref[p0, t, n % 2, rows, :] + e_ref[t, n % 2, p0, rows, :]
-                for t, n in zip(there, range(p0, p0 + KEPT))
-            ]
+            parts = []
+            for n in range(p0, p0 + KEPT):
+                there, q0 = n // 2, n % 2
+                first = z_ref[p0, lax.rem(row + there, ROWS), q0, rows, :]
+                second = got[there][q0, p0, rows, :] if there else z_ref[q0, row, p0, rows, :]
+                parts.append(first + second)
             sh, sl = halves(jnp.concatenate(parts, axis=0))
             total = dot3(wh, wl, sh, sl, NN).reshape(OCC, 8, VIRT)
             scale = 1.0 / d_ref[p0, :, rows, :]
@@ -197,17 +199,17 @@
             u_ref[p0, :, rows, :] = total * scale
 
 
-def kept_items(row, z, e, w, d):
-    shape = jax.ShapeDtypeStruct(d.shape, F32)
+def kept_items(row, z, *rest):
+    shape = jax.ShapeDtypeStruct(rest[-1].shape, F32)
     return pl.pallas_call(
         kept_kernel,
         out_shape=(shape, shape),
-        in_specs=[SMEM] + [VMEM] * 4,
+        in_specs=[SMEM] + [VMEM] * 7,
         out_specs=(VMEM, VMEM),
         compiler_params=pltpu.CompilerParams(vmem_limit_bytes=40 * 2**20),
-        cost_estimate=pl.CostEstimate(flops=2 * 10**9, bytes_accessed=12 * 10**6, transcendentals=0),
+        cost_estimate=pl.CostEstimate(flops=10**11, bytes_accessed=12 * 10**6, transcendentals=0),
         name="kept_items",
-    )(row, z, e, w, d)
+    )(row, z, *rest)
 
 
 def finish_kernel(row_ref, back_hbm, w_ref, u_hbm, r_hbm, o_ref, back, u, r, out, ins, outs):
@@ -284,10 +286,15 @@
     z = transform(mode, amplitudes[0], first_rotation, second_rotation)
     z = lax.all_to_all(z.reshape(COLS, WIDTH, VIRT), "occj", split_axis=0, concat_axis=0, tiled=True)
     z = z.reshape(2, ROWS, 2, WIDTH, VIRT)
-    e = lax.all_to_all(jnp.swapaxes(z, 0, 1), "occi", split_axis=0, concat_axis=0, tiled=True)
-    lost = lost_items(row_here, z, e)
+
+    def exchange(step):
+        out = lax.dynamic_index_in_dim(z, jnp.mod(row + step, ROWS), 1, keepdims=False)
+        return lax.ppermute(out, "occi", [(r, (r + step) % ROWS) for r in range(ROWS)])
+
+    got = {ROWS - step: exchange(step) for step in range(1, ROWS)}
+    lost = lost_items(row_here, z, got[7], got[6], got[5], got[4])
     back = lax.all_to_all(lost.reshape(COLS, WIDTH, HALF), "occj", split_axis=0, concat_axis=0, tiled=True)
-    u, r = kept_items(row_here, z, e, pair_weights, denominators)
+    u, r = kept_items(row_here, z, got[4], got[3], got[2], got[1], pair_weights, denominators)
     return finish(row_here, back, pair_weights, u, r)
 
 

time: 163 us -> 165 us (1.012)
  the two profiles are of different devices: /device:TPU:1 before, /device:TPU:49 now
where the time goes in v4:
time: 165 us
  waiting for transfers between devices  99.8 us (60%)
  starting transfers between devices  34.9 us (21%)
  Pallas kernels  22.3 us (14%)
  local copies, waits for them, and re-layouts  7.34 us (4%)
    all_to_all x1, waiting for transfers between devices, on_device(): lax.all_to_all(z.reshape(COLS, WIDTH, VIRT), 'occj', split_axis=0, concat...  51.4 us
    ppermute x7, waiting for transfers between devices, exchange(): lax.ppermute(out, 'occi', [(r, (r + step) % ROWS) for r in range(ROWS)])  24.3 us
    all_to_all x1, waiting for transfers between devices, on_device(): lax.all_to_all(lost.reshape(COLS, WIDTH, HALF), 'occj', split_axis=0, con...  24.1 us
    ppermute x7, starting transfers between devices, exchange(): lax.ppermute(out, 'occi', [(r, (r + step) % ROWS) for r in range(ROWS)])  12.8 us
    all_to_all x1, starting transfers between devices, on_device(): lax.all_to_all(z.reshape(COLS, WIDTH, VIRT), 'occj', split_axis=0, concat...  11.4 us
    all_to_all x1, starting transfers between devices, on_device(): lax.all_to_all(lost.reshape(COLS, WIDTH, HALF), 'occj', split_axis=0, con...  10.8 us
    pallas_call x1, Pallas kernels, transform(): pl.pallas_call(transform_kernel, out_shape=jax.ShapeDtypeStruct((VIRT, VI...  10.6 us
    unnamed x22, local copies, waits for them, and re-layouts  6.23 us
  transfers between devices with their start and end apart: 9, of which 6 were waited for; matrix products, arithmetic and copies ran while one was open for 0% of the time, Pallas kernels for 4%

profile of v4, /device:TPU:49, one launch (start us, length us, event | category | flops | bytes accessed | tf_op | source)
XLA Modules:
  0.0 164.7 jit_solution(10636472544448815748)
XLA Ops:
  0.0 10.6 %transform.1 = f32[768,768]{1,0:T(8,128)} custom-call(s32[1]{0:T(128)} %bitcast.1.mode_ref, f32[768,768]{1,0:T(8,128)} %bitcast.25, f32[768,768]{1,0:T(8,128)} %a_ref.1, f32[768,768]{1,0:T(8,128)} %b_ref.1), custom_call_target="tpu_custom_call" | custom-call | tf_op jit(solution)/shard_map/transform/pallas_call | solution.py:97
  10.7 11.4 %all-to-all-start = ((f32[32,24,768]{2,1,0:T(8,128)}), f32[32,24,768]{2,1,0:T(8,128)S(1)}, u32[]{:S(2)}, u32[]{:S(2)}) async-start(f32[32,24,768]{2,1,0:T(8,128)} %bitcast.23), calls=%async_computation | async-start | bytes 4718592 | tf_op jit(solution)/shard_map/all_to_all | solution.py:287
  22.1 51.4 %all-to-all-done = f32[32,24,768]{2,1,0:T(8,128)S(1)} async-done(((f32[32,24,768]{2,1,0:T(8,128)}), f32[32,24,768]{2,1,0:T(8,128)S(1)}, u32[]{:S(2)}, u32[]{:S(2)}) %all-to-all-start) | async-done | bytes 2359328 | tf_op jit(solution)/shard_map/all_to_all | solution.py:287
  73.5 1.1 dynamic-slice_bitcast_fusion
  74.6 6.8 %collective-permute-start.3 = (f32[2,2,24,768]{3,2,1,0:T(8,128)S(1)}, f32[2,2,24,768]{3,2,1,0:T(8,128)S(1)}, u32[]{:S(2)}, u32[]{:S(2)}) collective-permute-start(f32[2,2,24,768]{3,2,1,0:T(8,128)S(1)} %get-tuple-element.12), channel_id=1, source_target_pairs={{0,128},{32,160},{64,192},{96,224},{128,0},{160,32},{192,64},{224,... | collective-permute-start | bytes 884744 | tf_op jit(solution)/shard_map/ppermute | solution.py:292
  81.5 0.0 collective-permute-start
  81.5 1.4 collective-permute-start.1
  82.8 0.8 collective-permute-start.2
  83.7 2.0 %collective-permute-start.4 = (f32[2,2,24,768]{3,2,1,0:T(8,128)}, f32[2,2,24,768]{3,2,1,0:T(8,128)S(1)}, u32[]{:S(2)}, u32[]{:S(2)}) collective-permute-start(f32[2,2,24,768]{3,2,1,0:T(8,128)} %get-tuple-element.11), channel_id=1, source_target_pairs={{0,160},{32,192},{64,224},{96,0},{128,32},{160,64},{192,96},{224,1... | collective-permute-start | bytes 884744 | tf_op jit(solution)/shard_map/ppermute | solution.py:292
  85.6 1.8 %collective-permute-done.3.g4 = f32[2,2,24,768]{3,2,1,0:T(8,128)S(1)} collective-permute-done((f32[2,2,24,768]{3,2,1,0:T(8,128)S(1)}, f32[2,2,24,768]{3,2,1,0:T(8,128)S(1)}, u32[]{:S(2)}, u32[]{:S(2)}) %collective-permute-start.3) | collective-permute-done | bytes 294944 | tf_op jit(solution)/shard_map/ppermute | solution.py:292
  87.5 0.9 collective-permute-start.5
  88.4 0.4 collective-permute-done.g7
  88.8 0.8 collective-permute-start.6
  89.6 21.1 %collective-permute-done.1.g6 = f32[2,2,24,768]{3,2,1,0:T(8,128)S(1)} collective-permute-done((f32[2,2,24,768]{3,2,1,0:T(8,128)S(1)}, f32[2,2,24,768]{3,2,1,0:T(8,128)S(1)}, u32[]{:S(2)}, u32[]{:S(2)}) %collective-permute-start.1) | collective-permute-done | bytes 294944 | tf_op jit(solution)/shard_map/ppermute | solution.py:292
  110.7 0.9 collective-permute-done.2.g5
  111.6 0.0 copy-done.8
  111.6 0.0 copy-done.9
  111.6 0.7 copy-done.10
  112.4 0.0 copy-done
  112.4 3.1 %lost_items.1 = f32[768,384]{1,0:T(8,128)} custom-call(s32[1]{0:T(128)} %bitcast.row_ref, f32[2,8,2,24,768]{4,3,2,1,0:T(8,128)} %bitcast.21, f32[2,2,24,768]{3,2,1,0:T(8,128)} %copy-done.8, f32[2,2,24,768]{3,2,1,0:T(8,128)} %copy-done.9, f32[2,2,24,768]{3,2,1,0:T(8,128)} %copy-done.10, f32[2,2,24,768]{3,2,1,0:T(8,128)} %copy-done.4), custom_call_target="tpu_custom_call" | custom-call | tf_op jit(solution)/shard_map/lost_items/pallas_call | solution.py:148
  115.4 0.0 copy-start.1
  115.5 10.8 %all-to-all-start.1 = ((f32[32,24,384]{2,1,0:T(8,128)}), f32[32,24,384]{2,1,0:T(8,128)}, u32[]{:S(2)}, u32[]{:S(2)}) async-start(f32[32,24,384]{2,1,0:T(8,128)} %bitcast.24), calls=%async_computation.1 | async-start | bytes 2359296 | tf_op jit(solution)/shard_map/all_to_all | solution.py:296
  126.3 0.0 collective-permute-done.4.g3
  126.3 0.0 collective-permute-done.5.g2
  126.3 0.0 collective-permute-done.6.g1
  126.3 1.0 copy-done.5
  127.3 1.7 %copy-done.7 = f32[2,16,24,768]{3,2,1,0:T(8,128)S(1)} copy-done((f32[2,16,24,768]{3,2,1,0:T(8,128)S(1)}, f32[2,16,24,768]{3,2,1,0:T(8,128)}, u32[]{:S(2)}) %copy-start.7) | copy-done | bytes 2359320
  128.9 3.0 %kept_items.1 = (f32[2,16,24,768]{3,2,1,0:T(8,128)S(1)}, f32[2,16,24,768]{3,2,1,0:T(8,128)S(1)}) custom-call(s32[1]{0:T(128)} %bitcast.row_ref, f32[2,8,2,24,768]{4,3,2,1,0:T(8,128)S(1)} %bitcast.22, f32[2,2,24,768]{3,2,1,0:T(8,128)S(1)} %copy-done.5, f32[2,2,24,768]{3,2,1,0:T(8,128)S(1)} %collective-permute-done.4.g3, ...), custom_call_target="tpu_custom_call" | custom-call | flops 99999997952 | bytes 12000000 | tf_op jit(solution)/shard_map/kept_items/pallas_call | solution.py:204
  131.9 1.4 copy-done.2
  133.4 1.4 copy-done.3
  134.8 24.1 %all-to-all-done.1.back_hbm = f32[32,24,384]{2,1,0:T(8,128)} async-done(((f32[32,24,384]{2,1,0:T(8,128)}), f32[32,24,384]{2,1,0:T(8,128)}, u32[]{:S(2)}, u32[]{:S(2)}) %all-to-all-start.1) | async-done | bytes 1179680 | tf_op jit(solution)/shard_map/all_to_all | solution.py:296
  158.9 5.6 %finish.1 = f32[2,16,24,768]{3,2,1,0:T(8,128)} custom-call(s32[1]{0:T(128)} %bitcast.row_ref, f32[32,24,384]{2,1,0:T(8,128)} %all-to-all-done.1.back_hbm, f32[16,16]{1,0:T(8,128)} %w_ref.3, f32[2,16,24,768]{3,2,1,0:T(8,128)} %copy-done.2, f32[2,16,24,768]{3,2,1,0:T(8,128)} %copy-done.3), custom_call_target="tpu_custom_call" | custom-call | tf_op jit(solution)/shard_map/finish/pallas_call | solution.py:264
  (13 shorter events, 0.0 us)
Async XLA Ops:
  10.7 62.9 %all-to-all-start = ((f32[32,24,768]{2,1,0:T(8,128)}), f32[32,24,768]{2,1,0:T(8,128)S(1)}, u32[]{:S(2)}, u32[]{:S(2)}) async-start(f32[32,24,768]{2,1,0:T(8,128)} %bitcast.23), calls=%async_computation | async-start | bytes 4718592 | tf_op jit(solution)/shard_map/all_to_all | solution.py:287
  73.5 38.9 %copy-start = (f32[32,24,768]{2,1,0:T(8,128)}, f32[32,24,768]{2,1,0:T(8,128)S(1)}, u32[]{:S(2)}) copy-start(f32[32,24,768]{2,1,0:T(8,128)S(1)} %all-to-all-done) | copy-start | bytes 7077892
  74.6 12.8 %collective-permute-start.3 = (f32[2,2,24,768]{3,2,1,0:T(8,128)S(1)}, f32[2,2,24,768]{3,2,1,0:T(8,128)S(1)}, u32[]{:S(2)}, u32[]{:S(2)}) collective-permute-start(f32[2,2,24,768]{3,2,1,0:T(8,128)S(1)} %get-tuple-element.12), channel_id=1, source_target_pairs={{0,128},{32,160},{64,192},{96,224},{128,0},{160,32},{192,64},{224,... | collective-permute-start | bytes 884744 | tf_op jit(solution)/shard_map/ppermute | solution.py:292
  81.5 7.3 %collective-permute-start = (f32[2,2,24,768]{3,2,1,0:T(8,128)S(1)}, f32[2,2,24,768]{3,2,1,0:T(8,128)S(1)}, u32[]{:S(2)}, u32[]{:S(2)}) collective-permute-start(f32[2,2,24,768]{3,2,1,0:T(8,128)S(1)} %get-tuple-element.15), channel_id=1, source_target_pairs={{0,32},{32,64},{64,96},{96,128},{128,160},{160,192},{192,224},{224... | collective-permute-start | bytes 884744 | tf_op jit(solution)/shard_map/ppermute | solution.py:292
  81.5 29.2 %collective-permute-start.1 = (f32[2,2,24,768]{3,2,1,0:T(8,128)S(1)}, f32[2,2,24,768]{3,2,1,0:T(8,128)S(1)}, u32[]{:S(2)}, u32[]{:S(2)}) collective-permute-start(f32[2,2,24,768]{3,2,1,0:T(8,128)S(1)} %get-tuple-element.14), channel_id=1, source_target_pairs={{0,64},{32,96},{64,128},{96,160},{128,192},{160,224},{192,0},{224,... | collective-permute-start | bytes 884744 | tf_op jit(solution)/shard_map/ppermute | solution.py:292
  82.8 28.8 %collective-permute-start.2 = (f32[2,2,24,768]{3,2,1,0:T(8,128)S(1)}, f32[2,2,24,768]{3,2,1,0:T(8,128)S(1)}, u32[]{:S(2)}, u32[]{:S(2)}) collective-permute-start(f32[2,2,24,768]{3,2,1,0:T(8,128)S(1)} %get-tuple-element.13), channel_id=1, source_target_pairs={{0,96},{32,128},{64,160},{96,192},{128,224},{160,0},{192,32},{224,... | collective-permute-start | bytes 884744 | tf_op jit(solution)/shard_map/ppermute | solution.py:292
  83.7 42.6 %collective-permute-start.4 = (f32[2,2,24,768]{3,2,1,0:T(8,128)}, f32[2,2,24,768]{3,2,1,0:T(8,128)S(1)}, u32[]{:S(2)}, u32[]{:S(2)}) collective-permute-start(f32[2,2,24,768]{3,2,1,0:T(8,128)} %get-tuple-element.11), channel_id=1, source_target_pairs={{0,160},{32,192},{64,224},{96,0},{128,32},{160,64},{192,96},{224,1... | collective-permute-start | bytes 884744 | tf_op jit(solution)/shard_map/ppermute | solution.py:292
  87.5 24.9 %copy-start.4 = (f32[2,2,24,768]{3,2,1,0:T(8,128)}, f32[2,2,24,768]{3,2,1,0:T(8,128)S(1)}, u32[]{:S(2)}) copy-start(f32[2,2,24,768]{3,2,1,0:T(8,128)S(1)} %collective-permute-done.3.g4) | copy-start | bytes 884740
  87.5 38.8 %collective-permute-start.5 = (f32[2,2,24,768]{3,2,1,0:T(8,128)}, f32[2,2,24,768]{3,2,1,0:T(8,128)S(1)}, u32[]{:S(2)}, u32[]{:S(2)}) collective-permute-start(f32[2,2,24,768]{3,2,1,0:T(8,128)} %get-tuple-element.10), channel_id=1, source_target_pairs={{0,192},{32,224},{64,0},{96,32},{128,64},{160,96},{192,128},{224,1... | collective-permute-start | bytes 884744 | tf_op jit(solution)/shard_map/ppermute | solution.py:292
  88.8 22.9 %copy-start.8 = (f32[2,2,24,768]{3,2,1,0:T(8,128)}, f32[2,2,24,768]{3,2,1,0:T(8,128)S(1)}, u32[]{:S(2)}) copy-start(f32[2,2,24,768]{3,2,1,0:T(8,128)S(1)} %collective-permute-done.g7) | copy-start | bytes 884740
  88.8 37.5 %collective-permute-start.6 = (f32[2,2,24,768]{3,2,1,0:T(8,128)}, f32[2,2,24,768]{3,2,1,0:T(8,128)}, u32[]{:S(2)}, u32[]{:S(2)}) collective-permute-start(f32[2,2,24,768]{3,2,1,0:T(8,128)} %get-tuple-element.9), channel_id=1, source_target_pairs={{0,224},{32,0},{64,32},{96,64},{128,96},{160,128},{192,160},{224,1... | collective-permute-start | bytes 884744 | tf_op jit(solution)/shard_map/ppermute | solution.py:292
  110.7 1.0 copy-start.9
  111.6 0.7 copy-start.10
  112.4 13.9 %copy-start.6 = (f32[16,16]{1,0:T(8,128)S(1)}, f32[16,16]{1,0:T(8,128)}, u32[]{:S(2)}) copy-start(f32[16,16]{1,0:T(8,128)} %w_ref.3) | copy-start | bytes 3076
  115.4 10.9 %copy-start.1 = (f32[32,24,768]{2,1,0:T(8,128)S(1)}, f32[32,24,768]{2,1,0:T(8,128)}, u32[]{:S(2)}) copy-start(f32[32,24,768]{2,1,0:T(8,128)} %copy-done) | copy-start | bytes 7077892
  115.5 43.5 %all-to-all-start.1 = ((f32[32,24,384]{2,1,0:T(8,128)}), f32[32,24,384]{2,1,0:T(8,128)}, u32[]{:S(2)}, u32[]{:S(2)}) async-start(f32[32,24,384]{2,1,0:T(8,128)} %bitcast.24), calls=%async_computation.1 | async-start | bytes 2359296 | tf_op jit(solution)/shard_map/all_to_all | solution.py:296
  126.3 1.0 copy-start.5
  127.3 1.7 %copy-start.7 = (f32[2,16,24,768]{3,2,1,0:T(8,128)S(1)}, f32[2,16,24,768]{3,2,1,0:T(8,128)}, u32[]{:S(2)}) copy-start(f32[2,16,24,768]{3,2,1,0:T(8,128)} %d_ref.1) | copy-start | bytes 7077892
  131.9 1.4 copy-start.2
  133.4 1.4 copy-start.3

commit v5 on v4

--- a/solution.py
+++ b/solution.py
@@ -287,11 +287,18 @@
     z = lax.all_to_all(z.reshape(COLS, WIDTH, VIRT), "occj", split_axis=0, concat_axis=0, tiled=True)
     z = z.reshape(2, ROWS, 2, WIDTH, VIRT)
 
-    def exchange(step):
-        out = lax.dynamic_index_in_dim(z, jnp.mod(row + step, ROWS), 1, keepdims=False)
+    def leaving(step):
+        return lax.dynamic_index_in_dim(z, jnp.mod(row + step, ROWS), 1, keepdims=False)
+
+    def arriving(step, out):
         return lax.ppermute(out, "occi", [(r, (r + step) % ROWS) for r in range(ROWS)])
 
-    got = {ROWS - step: exchange(step) for step in range(1, ROWS)}
+    got = {ROWS - step: arriving(step, leaving(step)) for step in (1, 2, 3, 4)}
+    first, rest = lax.optimization_barrier(
+        ([got[n] for n in (7, 6, 5, 4)], [leaving(step) for step in (5, 6, 7)])
+    )
+    got.update(zip((7, 6, 5, 4), first))
+    got.update({ROWS - step: arriving(step, out) for step, out in zip((5, 6, 7), rest)})
     lost = lost_items(row_here, z, got[7], got[6], got[5], got[4])
     back = lax.all_to_all(lost.reshape(COLS, WIDTH, HALF), "occj", split_axis=0, concat_axis=0, tiled=True)
     u, r = kept_items(row_here, z, got[4], got[3], got[2], got[1], pair_weights, denominators)

time: 165 us -> 170 us (1.030)
  the two profiles are of different devices: /device:TPU:49 before, /device:TPU:1 now
where the time goes in v5:
time: 170 us
  waiting for transfers between devices  86.4 us (51%)
  starting transfers between devices  54 us (32%)
  Pallas kernels  22.3 us (13%)
  local copies, waits for them, and re-layouts  6.63 us (4%)
    all_to_all x1, waiting for transfers between devices, on_device(): lax.all_to_all(z.reshape(COLS, WIDTH, VIRT), 'occj', split_axis=0, concat...  55.8 us
    ppermute x7, starting transfers between devices, arriving(): lax.ppermute(out, 'occi', [(r, (r + step) % ROWS) for r in range(ROWS)])  30.8 us
    all_to_all x1, waiting for transfers between devices, on_device(): lax.all_to_all(lost.reshape(COLS, WIDTH, HALF), 'occj', split_axis=0, con...  23.3 us
    all_to_all x1, starting transfers between devices, on_device(): lax.all_to_all(z.reshape(COLS, WIDTH, VIRT), 'occj', split_axis=0, concat...  12.6 us
    pallas_call x1, Pallas kernels, transform(): pl.pallas_call(transform_kernel, out_shape=jax.ShapeDtypeStruct((VIRT, VI...  10.6 us
    all_to_all x1, starting transfers between devices, on_device(): lax.all_to_all(lost.reshape(COLS, WIDTH, HALF), 'occj', split_axis=0, con...  10.6 us
    ppermute x7, waiting for transfers between devices, arriving(): lax.ppermute(out, 'occi', [(r, (r + step) % ROWS) for r in range(ROWS)])  7.36 us
    pallas_call x1, Pallas kernels, finish(): pl.pallas_call(finish_kernel, out_shape=jax.ShapeDtypeStruct(u.shape, F32...  5.59 us
  transfers between devices with their start and end apart: 9, of which 7 were waited for; matrix products, arithmetic and copies ran while one was open for 0% of the time, Pallas kernels for 4%

profile of v5, /device:TPU:1, one launch (start us, length us, event | category | flops | bytes accessed | tf_op | source)
XLA Modules:
  0.0 169.7 jit_solution(15110121137532844392)
XLA Ops:
  0.0 10.6 %transform.1 = f32[768,768]{1,0:T(8,128)} custom-call(s32[1]{0:T(128)} %bitcast.1.mode_ref, f32[768,768]{1,0:T(8,128)} %bitcast.25, f32[768,768]{1,0:T(8,128)} %a_ref.1, f32[768,768]{1,0:T(8,128)} %b_ref.1), custom_call_target="tpu_custom_call" | custom-call | tf_op jit(solution)/shard_map/transform/pallas_call | solution.py:97
  10.7 12.6 %all-to-all-start = ((f32[32,24,768]{2,1,0:T(8,128)}), f32[32,24,768]{2,1,0:T(8,128)S(1)}, u32[]{:S(2)}, u32[]{:S(2)}) async-start(f32[32,24,768]{2,1,0:T(8,128)} %bitcast.23), calls=%async_computation | async-start | bytes 4718592 | tf_op jit(solution)/shard_map/all_to_all | solution.py:287
  23.4 55.8 %all-to-all-done = f32[32,24,768]{2,1,0:T(8,128)S(1)} async-done(((f32[32,24,768]{2,1,0:T(8,128)}), f32[32,24,768]{2,1,0:T(8,128)S(1)}, u32[]{:S(2)}, u32[]{:S(2)}) %all-to-all-start) | async-done | bytes 2359328 | tf_op jit(solution)/shard_map/all_to_all | solution.py:287
  79.1 1.1 dynamic-slice_bitcast_fusion
  80.2 1.3 collective-permute-start
  81.5 3.8 %collective-permute-start.1 = (f32[2,2,24,768]{3,2,1,0:T(8,128)S(1)}, f32[2,2,24,768]{3,2,1,0:T(8,128)S(1)}, u32[]{:S(2)}, u32[]{:S(2)}) collective-permute-start(f32[2,2,24,768]{3,2,1,0:T(8,128)S(1)} %get-tuple-element.28), channel_id=1, source_target_pairs={{0,64},{32,96},{64,128},{96,160},{128,192},{160,224},{192,0},{224,... | collective-permute-start | bytes 884744 | tf_op jit(solution)/shard_map/ppermute | solution.py:294
  85.4 0.8 collective-permute-start.2
  86.2 2.5 %collective-permute-start.3 = (f32[2,2,24,768]{3,2,1,0:T(8,128)S(1)}, f32[2,2,24,768]{3,2,1,0:T(8,128)S(1)}, u32[]{:S(2)}, u32[]{:S(2)}) collective-permute-start(f32[2,2,24,768]{3,2,1,0:T(8,128)S(1)} %get-tuple-element.26), channel_id=1, source_target_pairs={{0,128},{32,160},{64,192},{96,224},{128,0},{160,32},{192,64},{224,... | collective-permute-start | bytes 884744 | tf_op jit(solution)/shard_map/ppermute | solution.py:294
  88.6 6.3 %collective-permute-done.g7 = f32[2,2,24,768]{3,2,1,0:T(8,128)S(1)} collective-permute-done((f32[2,2,24,768]{3,2,1,0:T(8,128)S(1)}, f32[2,2,24,768]{3,2,1,0:T(8,128)S(1)}, u32[]{:S(2)}, u32[]{:S(2)}) %collective-permute-start) | collective-permute-done | bytes 294944 | tf_op jit(solution)/shard_map/ppermute | solution.py:294
  94.9 0.7 collective-permute-done.1.g6
  95.6 0.2 collective-permute-done.2.g5
  95.7 0.0 collective-permute-done.3.g4
  95.7 11.1 %collective-permute-start.4 = (f32[2,2,24,768]{3,2,1,0:T(8,128)}, f32[2,2,24,768]{3,2,1,0:T(8,128)S(1)}, u32[]{:S(2)}, u32[]{:S(2)}) collective-permute-start(f32[2,2,24,768]{3,2,1,0:T(8,128)} %get-tuple-element.18), channel_id=1, source_target_pairs={{0,160},{32,192},{64,224},{96,0},{128,32},{160,64},{192,96},{224,1... | collective-permute-start | bytes 884744 | tf_op jit(solution)/shard_map/ppermute | solution.py:294
  106.8 11.2 %collective-permute-start.5 = (f32[2,2,24,768]{3,2,1,0:T(8,128)}, f32[2,2,24,768]{3,2,1,0:T(8,128)S(1)}, u32[]{:S(2)}, u32[]{:S(2)}) collective-permute-start(f32[2,2,24,768]{3,2,1,0:T(8,128)} %get-tuple-element.19), channel_id=1, source_target_pairs={{0,192},{32,224},{64,0},{96,32},{128,64},{160,96},{192,128},{224,1... | collective-permute-start | bytes 884744 | tf_op jit(solution)/shard_map/ppermute | solution.py:294
  118.1 0.1 collective-permute-start.6
  118.2 0.0 copy-done.8
  118.2 0.0 copy-done.9
  118.2 0.0 copy-done.4
  118.2 0.0 copy-start.6
  118.2 3.1 %lost_items.1 = f32[768,384]{1,0:T(8,128)} custom-call(s32[1]{0:T(128)} %bitcast.row_ref, f32[2,8,2,24,768]{4,3,2,1,0:T(8,128)} %bitcast.21, f32[2,2,24,768]{3,2,1,0:T(8,128)} %copy-done.8, f32[2,2,24,768]{3,2,1,0:T(8,128)} %copy-done.9, f32[2,2,24,768]{3,2,1,0:T(8,128)} %copy-done.10, f32[2,2,24,768]{3,2,1,0:T(8,128)} %copy-done.4), custom_call_target="tpu_custom_call" | custom-call | tf_op jit(solution)/shard_map/lost_items/pallas_call | solution.py:148
  121.3 0.0 copy-start.1
  121.3 10.6 %all-to-all-start.1 = ((f32[32,24,384]{2,1,0:T(8,128)}), f32[32,24,384]{2,1,0:T(8,128)}, u32[]{:S(2)}, u32[]{:S(2)}) async-start(f32[32,24,384]{2,1,0:T(8,128)} %bitcast.24), calls=%async_computation.1 | async-start | bytes 2359296 | tf_op jit(solution)/shard_map/all_to_all | solution.py:303
  131.9 0.0 collective-permute-done.4.g3
  131.9 0.2 collective-permute-done.5.g2
  132.1 0.1 collective-permute-done.6.g1
  132.1 1.0 copy-done.5
  133.1 1.7 copy-done.7
  134.8 3.0 %kept_items.1 = (f32[2,16,24,768]{3,2,1,0:T(8,128)S(1)}, f32[2,16,24,768]{3,2,1,0:T(8,128)S(1)}) custom-call(s32[1]{0:T(128)} %bitcast.row_ref, f32[2,8,2,24,768]{4,3,2,1,0:T(8,128)S(1)} %bitcast.22, f32[2,2,24,768]{3,2,1,0:T(8,128)S(1)} %copy-done.5, f32[2,2,24,768]{3,2,1,0:T(8,128)S(1)} %collective-permute-done.4.g3, ...), custom_call_target="tpu_custom_call" | custom-call | flops 99999997952 | bytes 12000000 | tf_op jit(solution)/shard_map/kept_items/pallas_call | solution.py:204
  137.8 1.4 copy-done.2
  139.2 1.4 copy-done.3
  140.6 23.3 %all-to-all-done.1.back_hbm = f32[32,24,384]{2,1,0:T(8,128)} async-done(((f32[32,24,384]{2,1,0:T(8,128)}), f32[32,24,384]{2,1,0:T(8,128)}, u32[]{:S(2)}, u32[]{:S(2)}) %all-to-all-start.1) | async-done | bytes 1179680 | tf_op jit(solution)/shard_map/all_to_all | solution.py:303
  163.9 5.6 %finish.1 = f32[2,16,24,768]{3,2,1,0:T(8,128)} custom-call(s32[1]{0:T(128)} %bitcast.row_ref, f32[32,24,384]{2,1,0:T(8,128)} %all-to-all-done.1.back_hbm, f32[16,16]{1,0:T(8,128)} %w_ref.3, f32[2,16,24,768]{3,2,1,0:T(8,128)} %copy-done.2, f32[2,16,24,768]{3,2,1,0:T(8,128)} %copy-done.3), custom_call_target="tpu_custom_call" | custom-call | tf_op jit(solution)/shard_map/finish/pallas_call | solution.py:264
  (13 shorter events, 0.0 us)
Async XLA Ops:
  10.7 68.5 %all-to-all-start = ((f32[32,24,768]{2,1,0:T(8,128)}), f32[32,24,768]{2,1,0:T(8,128)S(1)}, u32[]{:S(2)}, u32[]{:S(2)}) async-start(f32[32,24,768]{2,1,0:T(8,128)} %bitcast.23), calls=%async_computation | async-start | bytes 4718592 | tf_op jit(solution)/shard_map/all_to_all | solution.py:287
  79.1 39.1 %copy-start = (f32[32,24,768]{2,1,0:T(8,128)}, f32[32,24,768]{2,1,0:T(8,128)S(1)}, u32[]{:S(2)}) copy-start(f32[32,24,768]{2,1,0:T(8,128)S(1)} %all-to-all-done) | copy-start | bytes 7077892
  80.2 14.7 %collective-permute-start = (f32[2,2,24,768]{3,2,1,0:T(8,128)S(1)}, f32[2,2,24,768]{3,2,1,0:T(8,128)S(1)}, u32[]{:S(2)}, u32[]{:S(2)}) collective-permute-start(f32[2,2,24,768]{3,2,1,0:T(8,128)S(1)} %get-tuple-element.29), channel_id=1, source_target_pairs={{0,32},{32,64},{64,96},{96,128},{128,160},{160,192},{192,224},{224... | collective-permute-start | bytes 884744 | tf_op jit(solution)/shard_map/ppermute | solution.py:294
  81.5 14.0 %collective-permute-start.1 = (f32[2,2,24,768]{3,2,1,0:T(8,128)S(1)}, f32[2,2,24,768]{3,2,1,0:T(8,128)S(1)}, u32[]{:S(2)}, u32[]{:S(2)}) collective-permute-start(f32[2,2,24,768]{3,2,1,0:T(8,128)S(1)} %get-tuple-element.28), channel_id=1, source_target_pairs={{0,64},{32,96},{64,128},{96,160},{128,192},{160,224},{192,0},{224,... | collective-permute-start | bytes 884744 | tf_op jit(solution)/shard_map/ppermute | solution.py:294
  85.4 10.3 %collective-permute-start.2 = (f32[2,2,24,768]{3,2,1,0:T(8,128)S(1)}, f32[2,2,24,768]{3,2,1,0:T(8,128)S(1)}, u32[]{:S(2)}, u32[]{:S(2)}) collective-permute-start(f32[2,2,24,768]{3,2,1,0:T(8,128)S(1)} %get-tuple-element.27), channel_id=1, source_target_pairs={{0,96},{32,128},{64,160},{96,192},{128,224},{160,0},{192,32},{224,... | collective-permute-start | bytes 884744 | tf_op jit(solution)/shard_map/ppermute | solution.py:294
  86.2 9.6 %collective-permute-start.3 = (f32[2,2,24,768]{3,2,1,0:T(8,128)S(1)}, f32[2,2,24,768]{3,2,1,0:T(8,128)S(1)}, u32[]{:S(2)}, u32[]{:S(2)}) collective-permute-start(f32[2,2,24,768]{3,2,1,0:T(8,128)S(1)} %get-tuple-element.26), channel_id=1, source_target_pairs={{0,128},{32,160},{64,192},{96,224},{128,0},{160,32},{192,64},{224,... | collective-permute-start | bytes 884744 | tf_op jit(solution)/shard_map/ppermute | solution.py:294
  94.9 23.3 %copy-start.8 = (f32[2,2,24,768]{3,2,1,0:T(8,128)}, f32[2,2,24,768]{3,2,1,0:T(8,128)S(1)}, u32[]{:S(2)}) copy-start(f32[2,2,24,768]{3,2,1,0:T(8,128)S(1)} %collective-permute-done.g7) | copy-start | bytes 884740
  95.6 22.6 %copy-start.9 = (f32[2,2,24,768]{3,2,1,0:T(8,128)}, f32[2,2,24,768]{3,2,1,0:T(8,128)S(1)}, u32[]{:S(2)}) copy-start(f32[2,2,24,768]{3,2,1,0:T(8,128)S(1)} %collective-permute-done.1.g6) | copy-start | bytes 884740
  95.7 22.5 %copy-start.10 = (f32[2,2,24,768]{3,2,1,0:T(8,128)}, f32[2,2,24,768]{3,2,1,0:T(8,128)S(1)}, u32[]{:S(2)}) copy-start(f32[2,2,24,768]{3,2,1,0:T(8,128)S(1)} %collective-permute-done.2.g5) | copy-start | bytes 884740
  95.7 22.5 %copy-start.4 = (f32[2,2,24,768]{3,2,1,0:T(8,128)}, f32[2,2,24,768]{3,2,1,0:T(8,128)S(1)}, u32[]{:S(2)}) copy-start(f32[2,2,24,768]{3,2,1,0:T(8,128)S(1)} %collective-permute-done.3.g4) | copy-start | bytes 884740
  95.7 36.1 %collective-permute-start.4 = (f32[2,2,24,768]{3,2,1,0:T(8,128)}, f32[2,2,24,768]{3,2,1,0:T(8,128)S(1)}, u32[]{:S(2)}, u32[]{:S(2)}) collective-permute-start(f32[2,2,24,768]{3,2,1,0:T(8,128)} %get-tuple-element.18), channel_id=1, source_target_pairs={{0,160},{32,192},{64,224},{96,0},{128,32},{160,64},{192,96},{224,1... | collective-permute-start | bytes 884744 | tf_op jit(solution)/shard_map/ppermute | solution.py:294
  106.8 25.2 %collective-permute-start.5 = (f32[2,2,24,768]{3,2,1,0:T(8,128)}, f32[2,2,24,768]{3,2,1,0:T(8,128)S(1)}, u32[]{:S(2)}, u32[]{:S(2)}) collective-permute-start(f32[2,2,24,768]{3,2,1,0:T(8,128)} %get-tuple-element.19), channel_id=1, source_target_pairs={{0,192},{32,224},{64,0},{96,32},{128,64},{160,96},{192,128},{224,1... | collective-permute-start | bytes 884744 | tf_op jit(solution)/shard_map/ppermute | solution.py:294
  118.1 14.1 %collective-permute-start.6 = (f32[2,2,24,768]{3,2,1,0:T(8,128)}, f32[2,2,24,768]{3,2,1,0:T(8,128)}, u32[]{:S(2)}, u32[]{:S(2)}) collective-permute-start(f32[2,2,24,768]{3,2,1,0:T(8,128)} %get-tuple-element.20), channel_id=1, source_target_pairs={{0,224},{32,0},{64,32},{96,64},{128,96},{160,128},{192,160},{224,1... | collective-permute-start | bytes 884744 | tf_op jit(solution)/shard_map/ppermute | solution.py:294
  118.2 13.9 %copy-start.6 = (f32[16,16]{1,0:T(8,128)S(1)}, f32[16,16]{1,0:T(8,128)}, u32[]{:S(2)}) copy-start(f32[16,16]{1,0:T(8,128)} %w_ref.3) | copy-start | bytes 3076
  121.3 10.9 %copy-start.1 = (f32[32,24,768]{2,1,0:T(8,128)S(1)}, f32[32,24,768]{2,1,0:T(8,128)}, u32[]{:S(2)}) copy-start(f32[32,24,768]{2,1,0:T(8,128)} %copy-done) | copy-start | bytes 7077892
  121.3 42.6 %all-to-all-start.1 = ((f32[32,24,384]{2,1,0:T(8,128)}), f32[32,24,384]{2,1,0:T(8,128)}, u32[]{:S(2)}, u32[]{:S(2)}) async-start(f32[32,24,384]{2,1,0:T(8,128)} %bitcast.24), calls=%async_computation.1 | async-start | bytes 2359296 | tf_op jit(solution)/shard_map/all_to_all | solution.py:303
  132.1 1.0 copy-start.5
  133.1 1.7 copy-start.7
  137.8 1.4 copy-start.2
  139.2 1.4 copy-start.3

commit v6 on v3

--- a/solution.py
+++ b/solution.py
@@ -107,33 +107,14 @@
     )(mode, t, a, b)
 
 
-STEPS = (4, 5, 6, 7, 0)
-
-
-def lost_kernel(row_ref, z_hbm, e_hbm, o_ref, own, other, stage, turned, ins, outs):
+def lost_kernel(row_ref, z_ref, e_ref, o_ref, stage, turned, outs):
     row = row_ref[0]
-    loads = []
-    for i, step in enumerate(STEPS[:4]):
-        there = lax.rem(row + step, ROWS)
-        loads.append(
-            [pltpu.make_async_copy(z_hbm.at[p0, there], own.at[p0, i], ins.at[i, p0]) for p0 in range(2)]
-            + [pltpu.make_async_copy(e_hbm.at[there], other.at[i], ins.at[i, 2])]
-        )
-    loads.append([pltpu.make_async_copy(z_hbm.at[p0, row, 1 - p0], own.at[p0, 4, 1 - p0], ins.at[4, p0]) for p0 in range(2)])
-    for group in loads:
-        for load in group:
-            load.start()
-    for i, group in enumerate(loads):
-        for load in group:
-            load.wait()
-        for p0 in range(2):
-            for m in range(LOST):
-                partner = 8 + p0 + m
-                if (partner // 2) % ROWS == STEPS[i]:
-                    q0 = partner % 2
-                    second = own[1 - p0, i, p0] if i == 4 else other[i, q0, p0]
-                    at = (p0 * LOST + m) * WIDTH
-                    stage[at : at + WIDTH, :] = own[p0, i, q0] + second
+    for p0 in range(2):
+        for m in range(LOST):
+            partner = 8 + p0 + m
+            there, q0 = lax.rem(row + (partner // 2) % ROWS, ROWS), partner % 2
+            at = (p0 * LOST + m) * WIDTH
+            stage[at : at + WIDTH, :] = z_ref[p0, there, q0] + e_ref[there, q0, p0]
     sends = []
     for i in range(PARTS):
         rows = slice(i * CHUNK, (i + 1) * CHUNK)
@@ -148,17 +129,14 @@
     return pl.pallas_call(
         lost_kernel,
         out_shape=jax.ShapeDtypeStruct((VIRT, HALF), F32),
-        in_specs=[SMEM, HBM, HBM],
+        in_specs=[SMEM, VMEM, VMEM],
         out_specs=HBM,
         scratch_shapes=[
-            pltpu.VMEM((2, 5, 2, WIDTH, VIRT), F32),
-            pltpu.VMEM((4, 2, 2, WIDTH, VIRT), F32),
             pltpu.VMEM((HALF, VIRT), F32),
             pltpu.VMEM((VIRT, HALF), F32),
-            pltpu.SemaphoreType.DMA((5, 3)),
             pltpu.SemaphoreType.DMA((PARTS,)),
         ],
-        compiler_params=pltpu.CompilerParams(vmem_limit_bytes=63_500_000),
+        compiler_params=pltpu.CompilerParams(vmem_limit_bytes=40_000_000),
         name="lost_items",
     )(row, z, e)
 
@@ -210,16 +188,15 @@
     )(row, z, e, w, d)
 
 
-def finish_kernel(row_ref, back_hbm, w_ref, u_hbm, r_hbm, o_ref, back, u, r, out, ins, outs):
+def finish_kernel(row_ref, back, w_ref, u_hbm, r_hbm, o_ref, u, r, out, ins, outs):
     row = row_ref[0]
     groups = [slice(g * 8, (g + 1) * 8) for g in range(WIDTH // 8)]
     loads = []
     for g, rows in enumerate(groups):
         loads.append(
             [
-                pltpu.make_async_copy(back_hbm.at[:, rows], back.at[:, rows], ins.at[0, g]),
-                pltpu.make_async_copy(u_hbm.at[:, :, rows], u.at[:, :, rows], ins.at[1, g]),
-                pltpu.make_async_copy(r_hbm.at[:, :, rows], r.at[:, :, rows], ins.at[2, g]),
+                pltpu.make_async_copy(u_hbm.at[:, :, rows], u.at[:, :, rows], ins.at[0, g]),
+                pltpu.make_async_copy(r_hbm.at[:, :, rows], r.at[:, :, rows], ins.at[1, g]),
             ]
         )
         for load in loads[-1]:
@@ -232,7 +209,6 @@
     group = lax.broadcasted_iota(jnp.int32, (8, HALF), 1) // WIDTH
     sends = []
     for g, rows in enumerate(groups):
-        loads[g][0].wait()
         for half in range(2):
             lanes = slice(half * HALF, (half + 1) * HALF)
             x = [back[half * 16 + c, rows, :] for c in range(16)]
@@ -244,7 +220,7 @@
                         x[c] = jnp.where(upper, pltpu.roll(high, bit * WIDTH, 1), low)
                         x[c + bit] = jnp.where(upper, high, pltpu.roll(low, HALF - bit * WIDTH, 1))
             if half == 0:
-                for load in loads[g][1:]:
+                for load in loads[g]:
                     load.wait()
             for p0 in range(2):
                 sh, sl = halves(jnp.concatenate(x[p0 * LOST : (p0 + 1) * LOST], axis=0))
@@ -262,12 +238,11 @@
     return pl.pallas_call(
         finish_kernel,
         out_shape=jax.ShapeDtypeStruct(u.shape, F32),
-        in_specs=[SMEM, HBM, VMEM, HBM, HBM],
+        in_specs=[SMEM, VMEM, VMEM, HBM, HBM],
         out_specs=HBM,
-        scratch_shapes=[pltpu.VMEM(back.shape, F32)]
-        + [pltpu.VMEM(u.shape, F32)] * 3
-        + [pltpu.SemaphoreType.DMA((3, WIDTH // 8)), pltpu.SemaphoreType.DMA((WIDTH // 8,))],
-        compiler_params=pltpu.CompilerParams(vmem_limit_bytes=62_500_000),
+        scratch_shapes=[pltpu.VMEM(u.shape, F32)] * 3
+        + [pltpu.SemaphoreType.DMA((2, WIDTH // 8)), pltpu.SemaphoreType.DMA((WIDTH // 8,))],
+        compiler_params=pltpu.CompilerParams(vmem_limit_bytes=54_000_000),
         name="finish",
     )(row, back, w, u, r)
 

time: 163 us -> 160 us (0.982)
  Pallas kernels: 21.3 us -> 18.2 us
    pallas_call x1, Pallas kernels: 3.06 us -> 1.19 us  [lost_items(): pl.pallas_call(lost_kernel, out_shape=jax.ShapeDtypeStruct((VIRT, HALF),...]
where the time goes in v6:
time: 160 us; the launch traced here: 159 us
  blocking collectives  104 us (65%)
  waiting for transfers between devices  22.9 us (14%)
  Pallas kernels  18.2 us (11%)
  local copies, waits for them, and re-layouts  7.58 us (5%)
  starting transfers between devices  6.57 us (4%)
    all_to_all x1, blocking collectives, on_device(): lax.all_to_all(z.reshape(COLS, WIDTH, VIRT), 'occj', split_axis=0, concat...  70.5 us
    all_to_all x1, blocking collectives, on_device(): lax.all_to_all(jnp.swapaxes(z, 0, 1), 'occi', split_axis=0, concat_axis=0...  33.5 us
    all_to_all x1, waiting for transfers between devices, on_device(): lax.all_to_all(lost.reshape(COLS, WIDTH, HALF), 'occj', split_axis=0, con...  22.9 us
    pallas_call x1, Pallas kernels, transform(): pl.pallas_call(transform_kernel, out_shape=jax.ShapeDtypeStruct((VIRT, VI...  10.6 us
    unnamed x14, local copies, waits for them, and re-layouts  7.43 us
    all_to_all x1, starting transfers between devices, on_device(): lax.all_to_all(lost.reshape(COLS, WIDTH, HALF), 'occj', split_axis=0, con...  6.57 us
    pallas_call x1, Pallas kernels, finish(): pl.pallas_call(finish_kernel, out_shape=jax.ShapeDtypeStruct(u.shape, F32...  4.33 us
  transfers between devices with their start and end apart: 1, of which 1 were waited for; matrix products, arithmetic and copies ran while one was open for 0% of the time, Pallas kernels for 1%

profile of v6, /device:TPU:1, one launch (start us, length us, event | category | flops | bytes accessed | tf_op | source)
XLA Modules:
  0.0 159.3 jit_solution(12243508282452718032)
XLA Ops:
  0.0 10.6 %transform.1 = f32[768,768]{1,0:T(8,128)} custom-call(s32[1]{0:T(128)} %bitcast.1.mode_ref, f32[768,768]{1,0:T(8,128)} %bitcast.15, f32[768,768]{1,0:T(8,128)} %a_ref.1, f32[768,768]{1,0:T(8,128)} %b_ref.1), custom_call_target="tpu_custom_call" | custom-call | tf_op jit(solution)/shard_map/transform/pallas_call | solution.py:97
  10.7 70.5 %all_to_all.15 = f32[32,24,768]{2,1,0:T(8,128)S(1)} all-to-all(f32[32,24,768]{2,1,0:T(8,128)} %bitcast.14), channel_id=1, replica_groups=mesh['occi'=8,'occj'=32] {'occj'}, dimensions={0} | all-to-all | bytes 4718592 | tf_op jit(solution)/shard_map/all_to_all | solution.py:260
  81.2 0.2 copy.10
  81.3 33.5 %all_to_all.16.e_ref = f32[8,2,2,24,768]{4,3,2,1,0:T(8,128)S(1)} all-to-all(f32[8,2,2,24,768]{4,3,2,1,0:T(8,128)S(1)} %bitcast.13), channel_id=1, replica_groups=mesh['occi'=8,'occj'=32] {'occi'}, dimensions={0} | all-to-all | bytes 4718592 | tf_op jit(solution)/shard_map/all_to_all | solution.py:262
  114.8 0.0 copy-start
  114.8 1.2 lost_items.1
  116.0 0.2 copy-done
  116.2 0.0 copy-start.2
  116.2 1.1 copy-done.2
  117.3 0.0 copy-start.5
  117.3 6.6 %all-to-all-start.2 = ((f32[32,24,384]{2,1,0:T(8,128)}), f32[32,24,384]{2,1,0:T(8,128)S(1)}, u32[]{:S(2)}, u32[]{:S(2)}) async-start(f32[32,24,384]{2,1,0:T(8,128)} %bitcast.12), calls=%async_computation.2 | async-start | bytes 2359296 | tf_op jit(solution)/shard_map/all_to_all | solution.py:264
  123.9 0.0 copy-done.5
  123.9 0.0 copy-start.1
  123.9 1.7 %copy-done.1 = f32[8,2,2,24,768]{4,3,2,1,0:T(8,128)S(1)} copy-done((f32[8,2,2,24,768]{4,3,2,1,0:T(8,128)S(1)}, f32[8,2,2,24,768]{4,3,2,1,0:T(8,128)}, u32[]{:S(2)}) %copy-start.1) | copy-done | bytes 2359320
  125.6 0.0 copy-start.6
  125.6 1.7 %copy-done.6 = f32[2,16,24,768]{3,2,1,0:T(8,128)S(1)} copy-done((f32[2,16,24,768]{3,2,1,0:T(8,128)S(1)}, f32[2,16,24,768]{3,2,1,0:T(8,128)}, u32[]{:S(2)}) %copy-start.6) | copy-done | bytes 2359320
  127.2 2.0 %kept_items.1 = (f32[2,16,24,768]{3,2,1,0:T(8,128)S(1)}, f32[2,16,24,768]{3,2,1,0:T(8,128)S(1)}) custom-call(s32[1]{0:T(128)} %bitcast.row_ref, f32[2,8,2,24,768]{4,3,2,1,0:T(8,128)S(1)} %bitcast.11, f32[8,2,2,24,768]{4,3,2,1,0:T(8,128)S(1)} %copy-done.1, f32[16,16]{1,0:T(8,128)S(1)} %copy-done.5, f32[2,16,24,768]{3,2,1,0:T(8,128)S(1)} %copy-done.6), custom_call_target="tpu_custom_call" | custom-call | flops 2000000000 | bytes 12000000 | tf_op jit(solution)/shard_map/kept_items/pallas_call | solution.py:180
  129.2 0.0 copy-start.3
  129.2 1.4 copy-done.3
  130.7 0.0 copy-start.4
  130.7 1.4 copy-done.4
  132.1 22.9 %all-to-all-done.2.back = f32[32,24,384]{2,1,0:T(8,128)S(1)} async-done(((f32[32,24,384]{2,1,0:T(8,128)}), f32[32,24,384]{2,1,0:T(8,128)S(1)}, u32[]{:S(2)}, u32[]{:S(2)}) %all-to-all-start.2) | async-done | bytes 1179680 | tf_op jit(solution)/shard_map/all_to_all | solution.py:264
  155.0 4.3 %finish.1 = f32[2,16,24,768]{3,2,1,0:T(8,128)} custom-call(s32[1]{0:T(128)} %bitcast.row_ref, f32[32,24,384]{2,1,0:T(8,128)S(1)} %all-to-all-done.2.back, f32[16,16]{1,0:T(8,128)S(1)} %copy-done.5, f32[2,16,24,768]{3,2,1,0:T(8,128)} %copy-done.3, f32[2,16,24,768]{3,2,1,0:T(8,128)} %copy-done.4), custom_call_target="tpu_custom_call" | custom-call | tf_op jit(solution)/shard_map/finish/pallas_call | solution.py:238
Async XLA Ops:
  114.8 1.4 copy-start
  116.2 1.1 copy-start.2
  117.3 6.6 %copy-start.5 = (f32[16,16]{1,0:T(8,128)S(1)}, f32[16,16]{1,0:T(8,128)}, u32[]{:S(2)}) copy-start(f32[16,16]{1,0:T(8,128)} %w_ref.3) | copy-start | bytes 3076
  117.3 37.7 %all-to-all-start.2 = ((f32[32,24,384]{2,1,0:T(8,128)}), f32[32,24,384]{2,1,0:T(8,128)S(1)}, u32[]{:S(2)}, u32[]{:S(2)}) async-start(f32[32,24,384]{2,1,0:T(8,128)} %bitcast.12), calls=%async_computation.2 | async-start | bytes 2359296 | tf_op jit(solution)/shard_map/all_to_all | solution.py:264
  123.9 1.7 %copy-start.1 = (f32[8,2,2,24,768]{4,3,2,1,0:T(8,128)S(1)}, f32[8,2,2,24,768]{4,3,2,1,0:T(8,128)}, u32[]{:S(2)}) copy-start(f32[8,2,2,24,768]{4,3,2,1,0:T(8,128)} %copy-done) | copy-start | bytes 7077892
  125.6 1.7 %copy-start.6 = (f32[2,16,24,768]{3,2,1,0:T(8,128)S(1)}, f32[2,16,24,768]{3,2,1,0:T(8,128)}, u32[]{:S(2)}) copy-start(f32[2,16,24,768]{3,2,1,0:T(8,128)} %d_ref.1) | copy-start | bytes 7077892
  129.2 1.4 copy-start.3
  130.7 1.4 copy-start.4

commit v7 on v6

--- a/solution.py
+++ b/solution.py
@@ -36,7 +36,7 @@
     return one(lh, rh) + (one(lh, rl) + one(ll, rh))
 
 
-def transform_kernel(mode_ref, t_ref, a_ref, b_ref, z_ref, t, a, b, z, t3, a3, pair, ins, outs):
+def transform_kernel(mode_ref, t_ref, a_ref, b_ref, z, t, a, b, t3, a3, pair, ins):
     mode = mode_ref[0]
     mine = jnp.where(mode == 0, 1, 0)
     chunks = [slice(i * CHUNK, (i + 1) * CHUNK) for i in range(PARTS)]
@@ -69,13 +69,8 @@
     for load, r in zip(loads[2], chunks):
         load.wait()
         put(1 - mine, r, b[r, :], mode != 0)
-    sends = [pltpu.make_async_copy(z.at[r], z_ref.at[r], outs.at[i]) for i, r in enumerate(chunks)]
-    for send, r in zip(sends, chunks):
+    for r in chunks:
         z[r, :] = lax.dot_general(pair[0, r, :], pair[1], NT, preferred_element_type=F32)
-
-        @pl.when(mode != 2)
-        def _():
-            send.start()
 
     @pl.when(mode == 2)
     def _():
@@ -86,11 +81,6 @@
                 z[i, j] = mean
                 if i != j:
                     z[j, i] = mean.T
-        for send in sends:
-            send.start()
-
-    for send in sends:
-        send.wait()
 
 
 def transform(mode, t, a, b):
@@ -98,16 +88,16 @@
         transform_kernel,
         out_shape=jax.ShapeDtypeStruct((VIRT, VIRT), F32),
         in_specs=[SMEM, HBM, HBM, HBM],
-        out_specs=HBM,
-        scratch_shapes=[pltpu.VMEM((VIRT, VIRT), F32)] * 4
+        out_specs=VMEM,
+        scratch_shapes=[pltpu.VMEM((VIRT, VIRT), F32)] * 3
         + [pltpu.VMEM((3 * VIRT, VIRT), BF16), pltpu.VMEM((VIRT, 3 * VIRT), BF16), pltpu.VMEM((2, VIRT, 3 * VIRT), BF16)]
-        + [pltpu.SemaphoreType.DMA((3, PARTS)), pltpu.SemaphoreType.DMA((PARTS,))],
-        compiler_params=pltpu.CompilerParams(vmem_limit_bytes=63_500_000),
+        + [pltpu.SemaphoreType.DMA((3, PARTS))],
+        compiler_params=pltpu.CompilerParams(vmem_limit_bytes=54_000_000),
         name="transform",
     )(mode, t, a, b)
 
 
-def lost_kernel(row_ref, z_ref, e_ref, o_ref, stage, turned, outs):
+def lost_kernel(row_ref, z_ref, e_ref, o_ref, stage):
     row = row_ref[0]
     for p0 in range(2):
         for m in range(LOST):
@@ -115,14 +105,9 @@
             there, q0 = lax.rem(row + (partner // 2) % ROWS, ROWS), partner % 2
             at = (p0 * LOST + m) * WIDTH
             stage[at : at + WIDTH, :] = z_ref[p0, there, q0] + e_ref[there, q0, p0]
-    sends = []
     for i in range(PARTS):
         rows = slice(i * CHUNK, (i + 1) * CHUNK)
-        turned[rows, :] = stage[:, rows].T
-        sends.append(pltpu.make_async_copy(turned.at[rows], o_ref.at[rows], outs.at[i]))
-        sends[-1].start()
-    for send in sends:
-        send.wait()
+        o_ref[rows, :] = stage[:, rows].T
 
 
 def lost_items(row, z, e):
@@ -130,13 +115,9 @@
         lost_kernel,
         out_shape=jax.ShapeDtypeStruct((VIRT, HALF), F32),
         in_specs=[SMEM, VMEM, VMEM],
-        out_specs=HBM,
-        scratch_shapes=[
-            pltpu.VMEM((HALF, VIRT), F32),
-            pltpu.VMEM((VIRT, HALF), F32),
-            pltpu.SemaphoreType.DMA((PARTS,)),
-        ],
-        compiler_params=pltpu.CompilerParams(vmem_limit_bytes=40_000_000),
+        out_specs=VMEM,
+        scratch_shapes=[pltpu.VMEM((HALF, VIRT), F32)],
+        compiler_params=pltpu.CompilerParams(vmem_limit_bytes=48_000_000),
         name="lost_items",
     )(row, z, e)
 

time: 160 us -> 158 us (0.988)
  Pallas kernels: 18.2 us -> 16.4 us
where the time goes in v7:
time: 158 us
  blocking collectives  103 us (65%)
  waiting for transfers between devices  22.9 us (14%)
  Pallas kernels  16.4 us (10%)
  local copies, waits for them, and re-layouts  8.4 us (5%)
  starting transfers between devices  6.56 us (4%)
    all_to_all x1, blocking collectives, on_device(): lax.all_to_all(z.reshape(COLS, WIDTH, VIRT), 'occj', split_axis=0, concat...  70.7 us
    all_to_all x1, blocking collectives, on_device(): lax.all_to_all(jnp.swapaxes(z, 0, 1), 'occi', split_axis=0, concat_axis=0...  32.6 us
    all_to_all x1, waiting for transfers between devices, on_device(): lax.all_to_all(lost.reshape(COLS, WIDTH, HALF), 'occj', split_axis=0, con...  22.9 us
    pallas_call x1, Pallas kernels, transform(): pl.pallas_call(transform_kernel, out_shape=jax.ShapeDtypeStruct((VIRT, VI...  9.75 us
    unnamed x14, local copies, waits for them, and re-layouts  8.25 us
    all_to_all x1, starting transfers between devices, on_device(): lax.all_to_all(lost.reshape(COLS, WIDTH, HALF), 'occj', split_axis=0, con...  6.56 us
    pallas_call x1, Pallas kernels, finish(): pl.pallas_call(finish_kernel, out_shape=jax.ShapeDtypeStruct(u.shape, F32...  4.33 us
  transfers between devices with their start and end apart: 1, of which 1 were waited for; matrix products, arithmetic and copies ran while one was open for 0% of the time, Pallas kernels for 1%

profile of v7, /device:TPU:1, one launch (start us, length us, event | category | flops | bytes accessed | tf_op | source)
XLA Modules:
  0.0 157.7 jit_solution(3489413701966402366)
XLA Ops:
  0.0 9.7 %transform.1 = f32[768,768]{1,0:T(8,128)S(1)} custom-call(s32[1]{0:T(128)} %bitcast.1.mode_ref, f32[768,768]{1,0:T(8,128)} %bitcast.15, f32[768,768]{1,0:T(8,128)} %a_ref.1, f32[768,768]{1,0:T(8,128)} %b_ref.1), custom_call_target="tpu_custom_call" | custom-call | tf_op jit(solution)/shard_map/transform/pallas_call | solution.py:87
  9.8 70.7 %all_to_all.15 = f32[32,24,768]{2,1,0:T(8,128)S(1)} all-to-all(f32[32,24,768]{2,1,0:T(8,128)S(1)} %bitcast.12), channel_id=1, replica_groups=mesh['occi'=8,'occj'=32] {'occj'}, dimensions={0} | all-to-all | bytes 4718592 | tf_op jit(solution)/shard_map/all_to_all | solution.py:241
  80.5 0.2 copy.10
  80.6 32.6 %all_to_all.16.e_ref = f32[8,2,2,24,768]{4,3,2,1,0:T(8,128)S(1)} all-to-all(f32[8,2,2,24,768]{4,3,2,1,0:T(8,128)S(1)} %bitcast.14), channel_id=1, replica_groups=mesh['occi'=8,'occj'=32] {'occi'}, dimensions={0} | all-to-all | bytes 4718592 | tf_op jit(solution)/shard_map/all_to_all | solution.py:243
  113.2 0.0 copy-start
  113.2 0.4 lost_items.1
  113.6 1.0 copy-done
  114.6 0.0 copy-start.2
  114.6 1.1 copy-done.2
  115.7 0.0 copy-start.5
  115.7 6.6 %all-to-all-start.2 = ((f32[32,24,384]{2,1,0:T(8,128)}), f32[32,24,384]{2,1,0:T(8,128)S(1)}, u32[]{:S(2)}, u32[]{:S(2)}) async-start(f32[32,24,384]{2,1,0:T(8,128)} %bitcast.13), calls=%async_computation.2 | async-start | bytes 2359296 | tf_op jit(solution)/shard_map/all_to_all | solution.py:245
  122.3 0.0 copy-done.5
  122.3 0.0 copy-start.1
  122.3 1.7 %copy-done.1 = f32[8,2,2,24,768]{4,3,2,1,0:T(8,128)S(1)} copy-done((f32[8,2,2,24,768]{4,3,2,1,0:T(8,128)S(1)}, f32[8,2,2,24,768]{4,3,2,1,0:T(8,128)}, u32[]{:S(2)}) %copy-start.1) | copy-done | bytes 2359320
  123.9 0.0 copy-start.6
  123.9 1.7 %copy-done.6 = f32[2,16,24,768]{3,2,1,0:T(8,128)S(1)} copy-done((f32[2,16,24,768]{3,2,1,0:T(8,128)S(1)}, f32[2,16,24,768]{3,2,1,0:T(8,128)}, u32[]{:S(2)}) %copy-start.6) | copy-done | bytes 2359320
  125.6 2.0 %kept_items.1 = (f32[2,16,24,768]{3,2,1,0:T(8,128)S(1)}, f32[2,16,24,768]{3,2,1,0:T(8,128)S(1)}) custom-call(s32[1]{0:T(128)} %bitcast.row_ref, f32[2,8,2,24,768]{4,3,2,1,0:T(8,128)S(1)} %bitcast.11, f32[8,2,2,24,768]{4,3,2,1,0:T(8,128)S(1)} %copy-done.1, f32[16,16]{1,0:T(8,128)S(1)} %copy-done.5, f32[2,16,24,768]{3,2,1,0:T(8,128)S(1)} %copy-done.6), custom_call_target="tpu_custom_call" | custom-call | flops 2000000000 | bytes 12000000 | tf_op jit(solution)/shard_map/kept_items/pallas_call | solution.py:161
  127.6 0.0 copy-start.3
  127.6 1.4 copy-done.3
  129.0 0.0 copy-start.4
  129.0 1.4 copy-done.4
  130.4 22.9 %all-to-all-done.2.back = f32[32,24,384]{2,1,0:T(8,128)S(1)} async-done(((f32[32,24,384]{2,1,0:T(8,128)}), f32[32,24,384]{2,1,0:T(8,128)S(1)}, u32[]{:S(2)}, u32[]{:S(2)}) %all-to-all-start.2) | async-done | bytes 1179680 | tf_op jit(solution)/shard_map/all_to_all | solution.py:245
  153.4 4.3 %finish.1 = f32[2,16,24,768]{3,2,1,0:T(8,128)} custom-call(s32[1]{0:T(128)} %bitcast.row_ref, f32[32,24,384]{2,1,0:T(8,128)S(1)} %all-to-all-done.2.back, f32[16,16]{1,0:T(8,128)S(1)} %copy-done.5, f32[2,16,24,768]{3,2,1,0:T(8,128)} %copy-done.3, f32[2,16,24,768]{3,2,1,0:T(8,128)} %copy-done.4), custom_call_target="tpu_custom_call" | custom-call | tf_op jit(solution)/shard_map/finish/pallas_call | solution.py:219
Async XLA Ops:
  113.2 1.4 copy-start
  114.6 1.1 copy-start.2
  115.7 6.6 %copy-start.5 = (f32[16,16]{1,0:T(8,128)S(1)}, f32[16,16]{1,0:T(8,128)}, u32[]{:S(2)}) copy-start(f32[16,16]{1,0:T(8,128)} %w_ref.3) | copy-start | bytes 3076
  115.7 37.7 %all-to-all-start.2 = ((f32[32,24,384]{2,1,0:T(8,128)}), f32[32,24,384]{2,1,0:T(8,128)S(1)}, u32[]{:S(2)}, u32[]{:S(2)}) async-start(f32[32,24,384]{2,1,0:T(8,128)} %bitcast.13), calls=%async_computation.2 | async-start | bytes 2359296 | tf_op jit(solution)/shard_map/all_to_all | solution.py:245
  122.3 1.7 %copy-start.1 = (f32[8,2,2,24,768]{4,3,2,1,0:T(8,128)S(1)}, f32[8,2,2,24,768]{4,3,2,1,0:T(8,128)}, u32[]{:S(2)}) copy-start(f32[8,2,2,24,768]{4,3,2,1,0:T(8,128)} %copy-done) | copy-start | bytes 7077892
  123.9 1.7 %copy-start.6 = (f32[2,16,24,768]{3,2,1,0:T(8,128)S(1)}, f32[2,16,24,768]{3,2,1,0:T(8,128)}, u32[]{:S(2)}) copy-start(f32[2,16,24,768]{3,2,1,0:T(8,128)} %d_ref.1) | copy-start | bytes 7077892
  127.6 1.4 copy-start.3
  129.0 1.4 copy-start.4

commit v8 on v7

--- a/solution.py
+++ b/solution.py
@@ -60,15 +60,17 @@
             t3[n * VIRT + i * CHUNK : n * VIRT + (i + 1) * CHUNK, :] = x
     for load in loads[2]:
         load.start()
-    for load, r in zip(loads[1], chunks):
-        load.wait()
+    for i, r in enumerate(chunks):
+        loads[1][i].wait()
+        early = range(2 * (i - 1), min(2 * i, PARTS)) if i else ()
+        for j in early:
+            loads[2][j].wait()
         h, l = halves(a[r, :])
         for third, x in zip(thirds, (h, h, l)):
             a3[r, third] = x
+        for j in early:
+            put(1 - mine, chunks[j], b[chunks[j], :], mode != 0)
         put(mine, r, lax.dot_general(a3[r, :], t3[...], NN, preferred_element_type=F32), mode == 0)
-    for load, r in zip(loads[2], chunks):
-        load.wait()
-        put(1 - mine, r, b[r, :], mode != 0)
     for r in chunks:
         z[r, :] = lax.dot_general(pair[0, r, :], pair[1], NT, preferred_element_type=F32)
 
@@ -97,7 +99,7 @@
     )(mode, t, a, b)
 
 
-def lost_kernel(row_ref, z_ref, e_ref, o_ref, stage):
+def sums_kernel(row_ref, z_ref, e_ref, o_ref, s_ref, stage):
     row = row_ref[0]
     for p0 in range(2):
         for m in range(LOST):
@@ -108,17 +110,24 @@
     for i in range(PARTS):
         rows = slice(i * CHUNK, (i + 1) * CHUNK)
         o_ref[rows, :] = stage[:, rows].T
-
-
-def lost_items(row, z, e):
-    return pl.pallas_call(
-        lost_kernel,
-        out_shape=jax.ShapeDtypeStruct((VIRT, HALF), F32),
+    for p0 in range(2):
+        for m in range(KEPT):
+            there, q0 = lax.rem(row + (p0 + m) // 2, ROWS), (p0 + m) % 2
+            s_ref[p0, m] = z_ref[p0, there, q0] + e_ref[there, q0, p0]
+
+
+def row_sums(row, z, e):
+    return pl.pallas_call(
+        sums_kernel,
+        out_shape=(
+            jax.ShapeDtypeStruct((VIRT, HALF), F32),
+            jax.ShapeDtypeStruct((2, KEPT, WIDTH, VIRT), F32),
+        ),
         in_specs=[SMEM, VMEM, VMEM],
-        out_specs=VMEM,
+        out_specs=(VMEM, VMEM),
         scratch_shapes=[pltpu.VMEM((HALF, VIRT), F32)],
         compiler_params=pltpu.CompilerParams(vmem_limit_bytes=48_000_000),
-        name="lost_items",
+        name="row_sums",
     )(row, z, e)
 
 
@@ -137,36 +146,31 @@
     return halves(jnp.where(same, full, 0.0))
 
 
-def kept_kernel(row_ref, z_ref, e_ref, w_ref, d_ref, u_ref, r_ref):
+def kept_kernel(row_ref, s_ref, w_ref, d_ref, u_ref, r_ref):
     row = row_ref[0]
     count = jnp.where(row < ROWS // 2, 1.0, 0.0)
     for p0 in range(2):
         wh, wl = weights(w_ref, row, p0, KEPT, KEPT - 1, count)
         for g in range(WIDTH // 8):
             rows = slice(g * 8, (g + 1) * 8)
-            there = [lax.rem(row + n // 2, ROWS) for n in range(p0, p0 + KEPT)]
-            parts = [
-                z_ref[p0, t, n % 2, rows, :] + e_ref[t, n % 2, p0, rows, :]
-                for t, n in zip(there, range(p0, p0 + KEPT))
-            ]
-            sh, sl = halves(jnp.concatenate(parts, axis=0))
+            sh, sl = halves(s_ref[p0, :, rows, :].reshape(KEPT * 8, VIRT))
             total = dot3(wh, wl, sh, sl, NN).reshape(OCC, 8, VIRT)
             scale = 1.0 / d_ref[p0, :, rows, :]
             r_ref[p0, :, rows, :] = scale
             u_ref[p0, :, rows, :] = total * scale
 
 
-def kept_items(row, z, e, w, d):
+def kept_items(row, kept, w, d):
     shape = jax.ShapeDtypeStruct(d.shape, F32)
     return pl.pallas_call(
         kept_kernel,
         out_shape=(shape, shape),
-        in_specs=[SMEM] + [VMEM] * 4,
+        in_specs=[SMEM] + [VMEM] * 3,
         out_specs=(VMEM, VMEM),
         compiler_params=pltpu.CompilerParams(vmem_limit_bytes=40 * 2**20),
         cost_estimate=pl.CostEstimate(flops=2 * 10**9, bytes_accessed=12 * 10**6, transcendentals=0),
         name="kept_items",
-    )(row, z, e, w, d)
+    )(row, kept, w, d)
 
 
 def finish_kernel(row_ref, back, w_ref, u_hbm, r_hbm, o_ref, u, r, out, ins, outs):
@@ -241,9 +245,9 @@
     z = lax.all_to_all(z.reshape(COLS, WIDTH, VIRT), "occj", split_axis=0, concat_axis=0, tiled=True)
     z = z.reshape(2, ROWS, 2, WIDTH, VIRT)
     e = lax.all_to_all(jnp.swapaxes(z, 0, 1), "occi", split_axis=0, concat_axis=0, tiled=True)
-    lost = lost_items(row_here, z, e)
+    lost, kept = row_sums(row_here, z, e)
     back = lax.all_to_all(lost.reshape(COLS, WIDTH, HALF), "occj", split_axis=0, concat_axis=0, tiled=True)
-    u, r = kept_items(row_here, z, e, pair_weights, denominators)
+    u, r = kept_items(row_here, kept, pair_weights, denominators)
     return finish(row_here, back, pair_weights, u, r)
 
 

time: 158 us -> 158 us (level)
  local copies, waits for them, and re-layouts: 8.4 us -> 5.4 us
  waiting for transfers between devices: 22.9 us -> 24.9 us
    unnamed x14 -> x12, local copies, waits for them, and re-layouts: 8.25 us -> 5.2 us
    all_to_all x1, waiting for transfers between devices: 22.9 us -> 24.9 us  [on_device(): lax.all_to_all(lost.reshape(COLS, WIDTH, HALF), 'occj', split_axis=0, con...]
where the time goes in v8:
time: 158 us; the launch traced here: 157 us
  blocking collectives  103 us (65%)
  waiting for transfers between devices  24.9 us (16%)
  Pallas kernels  16.9 us (11%)
  starting transfers between devices  6.56 us (4%)
  local copies, waits for them, and re-layouts  5.4 us (3%)
    all_to_all x1, blocking collectives, on_device(): lax.all_to_all(z.reshape(COLS, WIDTH, VIRT), 'occj', split_axis=0, concat...  70.2 us
    all_to_all x1, blocking collectives, on_device(): lax.all_to_all(jnp.swapaxes(z, 0, 1), 'occi', split_axis=0, concat_axis=0...  33.1 us
    all_to_all x1, waiting for transfers between devices, on_device(): lax.all_to_all(lost.reshape(COLS, WIDTH, HALF), 'occj', split_axis=0, con...  24.9 us
    pallas_call x1, Pallas kernels, transform(): pl.pallas_call(transform_kernel, out_shape=jax.ShapeDtypeStruct((VIRT, VI...  9.11 us
    all_to_all x1, starting transfers between devices, on_device(): lax.all_to_all(lost.reshape(COLS, WIDTH, HALF), 'occj', split_axis=0, con...  6.56 us
    unnamed x12, local copies, waits for them, and re-layouts  5.2 us
    pallas_call x1, Pallas kernels, finish(): pl.pallas_call(finish_kernel, out_shape=jax.ShapeDtypeStruct(u.shape, F32...  4.33 us
  transfers between devices with their start and end apart: 1, of which 1 were waited for; matrix products, arithmetic and copies ran while one was open for 0% of the time, Pallas kernels for 1%

profile of v8, /device:TPU:1, one launch (start us, length us, event | category | flops | bytes accessed | tf_op | source)
XLA Modules:
  0.0 157.2 jit_solution(2113684110982166428)
XLA Ops:
  0.0 9.1 %transform.1 = f32[768,768]{1,0:T(8,128)S(1)} custom-call(s32[1]{0:T(128)} %bitcast.1.mode_ref, f32[768,768]{1,0:T(8,128)} %bitcast.13, f32[768,768]{1,0:T(8,128)} %a_ref.1, f32[768,768]{1,0:T(8,128)} %b_ref.1), custom_call_target="tpu_custom_call" | custom-call | tf_op jit(solution)/shard_map/transform/pallas_call | solution.py:89
  9.1 70.2 %all_to_all.15 = f32[32,24,768]{2,1,0:T(8,128)S(1)} all-to-all(f32[32,24,768]{2,1,0:T(8,128)S(1)} %bitcast.11), channel_id=1, replica_groups=mesh['occi'=8,'occj'=32] {'occj'}, dimensions={0} | all-to-all | bytes 4718592 | tf_op jit(solution)/shard_map/all_to_all | solution.py:245
  79.4 0.2 copy.9
  79.6 33.1 %all_to_all.16.e_ref = f32[8,2,2,24,768]{4,3,2,1,0:T(8,128)S(1)} all-to-all(f32[8,2,2,24,768]{4,3,2,1,0:T(8,128)S(1)} %bitcast.12), channel_id=1, replica_groups=mesh['occi'=8,'occj'=32] {'occi'}, dimensions={0} | all-to-all | bytes 4718592 | tf_op jit(solution)/shard_map/all_to_all | solution.py:247
  112.7 0.0 copy-start.3
  112.7 1.5 row_sums.1
  114.1 0.0 copy-start.4
  114.1 1.1 copy-done.4
  115.2 0.0 copy-start.2
  115.2 6.6 %all-to-all-start.2 = ((f32[32,24,384]{2,1,0:T(8,128)}), f32[32,24,384]{2,1,0:T(8,128)S(1)}, u32[]{:S(2)}, u32[]{:S(2)}) async-start(f32[32,24,384]{2,1,0:T(8,128)} %bitcast.6), calls=%async_computation.2 | async-start | bytes 2359296 | tf_op jit(solution)/shard_map/all_to_all | solution.py:249
  121.8 0.0 copy-done.3
  121.8 0.0 copy-done.2
  121.8 0.0 copy-start.5
  121.8 1.3 copy-done.5
  123.1 2.0 %kept_items.1 = (f32[2,16,24,768]{3,2,1,0:T(8,128)S(1)}, f32[2,16,24,768]{3,2,1,0:T(8,128)S(1)}) custom-call(s32[1]{0:T(128)} %bitcast.row_ref, f32[2,9,24,768]{3,2,1,0:T(8,128)S(1)} %copy-done.5, f32[16,16]{1,0:T(8,128)S(1)} %copy-done.2, f32[2,16,24,768]{3,2,1,0:T(8,128)S(1)} %copy-done.3), custom_call_target="tpu_custom_call" | custom-call | flops 2000000000 | bytes 12000000 | tf_op jit(solution)/shard_map/kept_items/pallas_call | solution.py:165
  125.2 0.0 copy-start
  125.2 1.4 copy-done
  126.6 0.0 copy-start.1
  126.6 1.4 copy-done.1
  128.0 24.9 %all-to-all-done.2.back = f32[32,24,384]{2,1,0:T(8,128)S(1)} async-done(((f32[32,24,384]{2,1,0:T(8,128)}), f32[32,24,384]{2,1,0:T(8,128)S(1)}, u32[]{:S(2)}, u32[]{:S(2)}) %all-to-all-start.2) | async-done | bytes 1179680 | tf_op jit(solution)/shard_map/all_to_all | solution.py:249
  152.9 4.3 %finish.1 = f32[2,16,24,768]{3,2,1,0:T(8,128)} custom-call(s32[1]{0:T(128)} %bitcast.row_ref, f32[32,24,384]{2,1,0:T(8,128)S(1)} %all-to-all-done.2.back, f32[16,16]{1,0:T(8,128)S(1)} %copy-done.2, f32[2,16,24,768]{3,2,1,0:T(8,128)} %copy-done, f32[2,16,24,768]{3,2,1,0:T(8,128)} %copy-done.1), custom_call_target="tpu_custom_call" | custom-call | tf_op jit(solution)/shard_map/finish/pallas_call | solution.py:223
Async XLA Ops:
  112.7 9.1 %copy-start.3 = (f32[2,16,24,768]{3,2,1,0:T(8,128)S(1)}, f32[2,16,24,768]{3,2,1,0:T(8,128)}, u32[]{:S(2)}) copy-start(f32[2,16,24,768]{3,2,1,0:T(8,128)} %d_ref.1) | copy-start | bytes 7077892
  114.1 1.1 copy-start.4
  115.2 6.6 %copy-start.2 = (f32[16,16]{1,0:T(8,128)S(1)}, f32[16,16]{1,0:T(8,128)}, u32[]{:S(2)}) copy-start(f32[16,16]{1,0:T(8,128)} %w_ref.3) | copy-start | bytes 3076
  115.2 37.7 %all-to-all-start.2 = ((f32[32,24,384]{2,1,0:T(8,128)}), f32[32,24,384]{2,1,0:T(8,128)S(1)}, u32[]{:S(2)}, u32[]{:S(2)}) async-start(f32[32,24,384]{2,1,0:T(8,128)} %bitcast.6), calls=%async_computation.2 | async-start | bytes 2359296 | tf_op jit(solution)/shard_map/all_to_all | solution.py:249
  121.8 1.3 copy-start.5
  125.2 1.4 copy-start
  126.6 1.4 copy-start.1

commit v9 on v8

--- a/solution.py
+++ b/solution.py
@@ -99,8 +99,9 @@
     )(mode, t, a, b)
 
 
-def sums_kernel(row_ref, z_ref, e_ref, o_ref, s_ref, stage):
+def sums_kernel(row_ref, z_ref, e_ref, o_hbm, s, stage, o, outs):
     row = row_ref[0]
+    sends = []
     for p0 in range(2):
         for m in range(LOST):
             partner = 8 + p0 + m
@@ -109,11 +110,15 @@
             stage[at : at + WIDTH, :] = z_ref[p0, there, q0] + e_ref[there, q0, p0]
     for i in range(PARTS):
         rows = slice(i * CHUNK, (i + 1) * CHUNK)
-        o_ref[rows, :] = stage[:, rows].T
+        o[rows, :] = stage[:, rows].T
+        sends.append(pltpu.make_async_copy(o.at[rows], o_hbm.at[rows], outs.at[i]))
+        sends[-1].start()
     for p0 in range(2):
         for m in range(KEPT):
             there, q0 = lax.rem(row + (p0 + m) // 2, ROWS), (p0 + m) % 2
-            s_ref[p0, m] = z_ref[p0, there, q0] + e_ref[there, q0, p0]
+            s[p0, m] = z_ref[p0, there, q0] + e_ref[there, q0, p0]
+    for copy in sends:
+        copy.wait()
 
 
 def row_sums(row, z, e):
@@ -124,8 +129,12 @@
             jax.ShapeDtypeStruct((2, KEPT, WIDTH, VIRT), F32),
         ),
         in_specs=[SMEM, VMEM, VMEM],
-        out_specs=(VMEM, VMEM),
-        scratch_shapes=[pltpu.VMEM((HALF, VIRT), F32)],
+        out_specs=(HBM, VMEM),
+        scratch_shapes=[
+            pltpu.VMEM((HALF, VIRT), F32),
+            pltpu.VMEM((VIRT, HALF), F32),
+            pltpu.SemaphoreType.DMA((PARTS,)),
+        ],
         compiler_params=pltpu.CompilerParams(vmem_limit_bytes=48_000_000),
         name="row_sums",
     )(row, z, e)

time: 158 us -> 157 us (level)
  no operation moved by 1% of the time
where the time goes in v9:
time: 157 us
  blocking collectives  103 us (66%)
  waiting for transfers between devices  24.9 us (16%)
  Pallas kernels  16.8 us (11%)
  starting transfers between devices  6.56 us (4%)
  local copies, waits for them, and re-layouts  5.39 us (3%)
    all_to_all x1, blocking collectives, on_device(): lax.all_to_all(z.reshape(COLS, WIDTH, VIRT), 'occj', split_axis=0, concat...  70.2 us
    all_to_all x1, blocking collectives, on_device(): lax.all_to_all(jnp.swapaxes(z, 0, 1), 'occi', split_axis=0, concat_axis=0...  33.1 us
    all_to_all x1, waiting for transfers between devices, on_device(): lax.all_to_all(lost.reshape(COLS, WIDTH, HALF), 'occj', split_axis=0, con...  24.9 us
    pallas_call x1, Pallas kernels, transform(): pl.pallas_call(transform_kernel, out_shape=jax.ShapeDtypeStruct((VIRT, VI...  9.11 us
    all_to_all x1, starting transfers between devices, on_device(): lax.all_to_all(lost.reshape(COLS, WIDTH, HALF), 'occj', split_axis=0, con...  6.56 us
    unnamed x12, local copies, waits for them, and re-layouts  5.2 us
    pallas_call x1, Pallas kernels, finish(): pl.pallas_call(finish_kernel, out_shape=jax.ShapeDtypeStruct(u.shape, F32...  4.33 us
  transfers between devices with their start and end apart: 1, of which 1 were waited for; matrix products, arithmetic and copies ran while one was open for 0% of the time, Pallas kernels for 1%

profile of v9, /device:TPU:1, one launch (start us, length us, event | category | flops | bytes accessed | tf_op | source)
XLA Modules:
  0.0 157.1 jit_solution(16707537592436397893)
XLA Ops:
  0.0 9.1 %transform.1 = f32[768,768]{1,0:T(8,128)S(1)} custom-call(s32[1]{0:T(128)} %bitcast.1.mode_ref, f32[768,768]{1,0:T(8,128)} %bitcast.13, f32[768,768]{1,0:T(8,128)} %a_ref.1, f32[768,768]{1,0:T(8,128)} %b_ref.1), custom_call_target="tpu_custom_call" | custom-call | tf_op jit(solution)/shard_map/transform/pallas_call | solution.py:89
  9.1 70.2 %all_to_all.15 = f32[32,24,768]{2,1,0:T(8,128)S(1)} all-to-all(f32[32,24,768]{2,1,0:T(8,128)S(1)} %bitcast.11), channel_id=1, replica_groups=mesh['occi'=8,'occj'=32] {'occj'}, dimensions={0} | all-to-all | bytes 4718592 | tf_op jit(solution)/shard_map/all_to_all | solution.py:254
  79.4 0.2 copy.9
  79.6 33.1 %all_to_all.16.e_ref = f32[8,2,2,24,768]{4,3,2,1,0:T(8,128)S(1)} all-to-all(f32[8,2,2,24,768]{4,3,2,1,0:T(8,128)S(1)} %bitcast.12), channel_id=1, replica_groups=mesh['occi'=8,'occj'=32] {'occi'}, dimensions={0} | all-to-all | bytes 4718592 | tf_op jit(solution)/shard_map/all_to_all | solution.py:256
  112.7 0.0 copy-start.3
  112.7 1.3 row_sums.1
  114.0 0.0 copy-start.4
  114.0 1.1 copy-done.4
  115.1 0.0 copy-start.2
  115.1 6.6 %all-to-all-start.2 = ((f32[32,24,384]{2,1,0:T(8,128)}), f32[32,24,384]{2,1,0:T(8,128)S(1)}, u32[]{:S(2)}, u32[]{:S(2)}) async-start(f32[32,24,384]{2,1,0:T(8,128)} %bitcast.6), calls=%async_computation.2 | async-start | bytes 2359296 | tf_op jit(solution)/shard_map/all_to_all | solution.py:258
  121.7 0.0 copy-done.3
  121.7 0.0 copy-done.2
  121.7 0.0 copy-start.5
  121.7 1.3 copy-done.5
  123.0 2.0 %kept_items.1 = (f32[2,16,24,768]{3,2,1,0:T(8,128)S(1)}, f32[2,16,24,768]{3,2,1,0:T(8,128)S(1)}) custom-call(s32[1]{0:T(128)} %bitcast.row_ref, f32[2,9,24,768]{3,2,1,0:T(8,128)S(1)} %copy-done.5, f32[16,16]{1,0:T(8,128)S(1)} %copy-done.2, f32[2,16,24,768]{3,2,1,0:T(8,128)S(1)} %copy-done.3), custom_call_target="tpu_custom_call" | custom-call | flops 2000000000 | bytes 12000000 | tf_op jit(solution)/shard_map/kept_items/pallas_call | solution.py:174
  125.0 0.0 copy-start
  125.1 1.4 copy-done
  126.5 0.0 copy-start.1
  126.5 1.4 copy-done.1
  127.9 24.9 %all-to-all-done.2.back = f32[32,24,384]{2,1,0:T(8,128)S(1)} async-done(((f32[32,24,384]{2,1,0:T(8,128)}), f32[32,24,384]{2,1,0:T(8,128)S(1)}, u32[]{:S(2)}, u32[]{:S(2)}) %all-to-all-start.2) | async-done | bytes 1179680 | tf_op jit(solution)/shard_map/all_to_all | solution.py:258
  152.8 4.3 %finish.1 = f32[2,16,24,768]{3,2,1,0:T(8,128)} custom-call(s32[1]{0:T(128)} %bitcast.row_ref, f32[32,24,384]{2,1,0:T(8,128)S(1)} %all-to-all-done.2.back, f32[16,16]{1,0:T(8,128)S(1)} %copy-done.2, f32[2,16,24,768]{3,2,1,0:T(8,128)} %copy-done, f32[2,16,24,768]{3,2,1,0:T(8,128)} %copy-done.1), custom_call_target="tpu_custom_call" | custom-call | tf_op jit(solution)/shard_map/finish/pallas_call | solution.py:232
Async XLA Ops:
  112.7 9.0 %copy-start.3 = (f32[2,16,24,768]{3,2,1,0:T(8,128)S(1)}, f32[2,16,24,768]{3,2,1,0:T(8,128)}, u32[]{:S(2)}) copy-start(f32[2,16,24,768]{3,2,1,0:T(8,128)} %d_ref.1) | copy-start | bytes 7077892
  114.0 1.1 copy-start.4
  115.1 6.6 %copy-start.2 = (f32[16,16]{1,0:T(8,128)S(1)}, f32[16,16]{1,0:T(8,128)}, u32[]{:S(2)}) copy-start(f32[16,16]{1,0:T(8,128)} %w_ref.3) | copy-start | bytes 3076
  115.1 37.7 %all-to-all-start.2 = ((f32[32,24,384]{2,1,0:T(8,128)}), f32[32,24,384]{2,1,0:T(8,128)S(1)}, u32[]{:S(2)}, u32[]{:S(2)}) async-start(f32[32,24,384]{2,1,0:T(8,128)} %bitcast.6), calls=%async_computation.2 | async-start | bytes 2359296 | tf_op jit(solution)/shard_map/all_to_all | solution.py:258
  121.7 1.3 copy-start.5
  125.0 1.4 copy-start
  126.5 1.4 copy-start.1
